TPU v7x, 256 devices: a whole 4x4x8 slice. The times are simulated.
256 devices in a mesh: grp: 2 (over z_lo), vocab: 32 (over z_hi, y, core), seq: 4 (over x).
Axes of the slice: x: 4, y: 4, z: 8 (z_hi: 4, z_lo: 2; z = z_hi * 2 + z_lo), core: 2. Of those that a mesh axis runs over, the one named last changes fastest.
Arguments:
- hidden_states: bfloat16 [2, 256, 8192], P('grp', 'seq', 'vocab'), may hold values from -128 to 127, as said below
- head_weights: bfloat16 [2, 8192, 81920], P('grp', None, ('vocab', 'seq')), may hold values from -8 to 7, as said below
- weight_scales: float32 [64, 81920], P(None, ('vocab', 'seq')), may hold values from 0.003 to 0.012
- token_scales: float32 [256], P('seq'), may hold values from 0.005 to 0.05
Outputs:
- row_grads: bfloat16 [2, 256, 8192], P('grp', 'seq', 'vocab')
- token_kl: float32 [256], replicated
Inputs may be any that keep to these rules, and one draw needn't show every extreme that they name: hidden_states[1] and head_weights[1] hold whole numbers. head_weights[1] holds int4 codes.
All inputs are finite; a program needn't handle non-finite values.
Results may differ from a plain program's by a relative error of at most 0.04.
Values may be sent and summed in bfloat16 or wider, within the bound.
No kernel may reach another device: no remote copies, remote signals or barrier semaphores. Data moves between devices by JAX's collectives and lax.ppermute only.
A program may use at most 128 MiB of HBM per device.

v0:
```python
import jax
import jax.numpy as jnp
from jax import lax
from jax.sharding import PartitionSpec as P

loss_scale = 1024.0


def swapped(value, axis, distance):
    return lax.ppermute(value, axis, [(i, i ^ 1 << distance) for i in range(lax.axis_size(axis))])


def body(hidden_states, head_weights, weight_scales, token_scales):
    quantized = lax.axis_index("grp") == 1
    row_factor = jnp.where(quantized, token_scales, 1.0)
    local_rows = (hidden_states[0].astype(jnp.float32) * row_factor[:, None]).astype(jnp.bfloat16)
    codes = head_weights[0]
    width, columns = codes.shape
    groups = weight_scales.shape[0]
    col_factor = jnp.where(quantized, weight_scales, 1.0)
    weights = (
        (
            codes.astype(jnp.float32).reshape(groups, width // groups, columns)
            * col_factor[:, None, :]
        )
        .reshape(width, columns)
        .astype(jnp.bfloat16)
    )
    rows = lax.all_gather(local_rows, "seq", axis=0, tiled=True)
    logits = jnp.dot(
        lax.all_gather(rows, "vocab", axis=1, tiled=True),
        weights,
        preferred_element_type=jnp.float32,
    )
    top = lax.pmax(jnp.max(logits, axis=1), ("vocab", "seq"))
    total = lax.psum(jnp.sum(jnp.exp(logits - top[:, None]), axis=1), ("vocab", "seq"))
    lse = top + jnp.log(total)
    own_logp = (logits - lse[:, None]).astype(jnp.bfloat16)
    other_logp = swapped(own_logp, "grp", 0)
    ref_lp = jnp.where(quantized, other_logp, own_logp).astype(jnp.float32)
    quant_lp = jnp.where(quantized, own_logp, other_logp).astype(jnp.float32)
    p_ref = jnp.exp(ref_lp)
    diff = ref_lp - quant_lp
    token_kl = lax.psum(jnp.sum(p_ref * diff, axis=1), ("vocab", "seq"))
    grad_ref = p_ref * (diff - token_kl[:, None])
    grad_quant = jnp.exp(quant_lp) - p_ref
    grad_logits = (loss_scale * jnp.where(quantized, grad_quant, grad_ref)).astype(jnp.bfloat16)
    partial_value = lax.dot_general(
        grad_logits, weights, (((1,), (1,)), ((), ())), preferred_element_type=jnp.float32
    )
    by_features = lax.psum_scatter(partial_value, "vocab", scatter_dimension=1, tiled=True)
    summed = lax.psum_scatter(by_features, "seq", scatter_dimension=0, tiled=True)
    return (summed.astype(jnp.bfloat16)[None], token_kl)


def solution(mesh):
    return jax.shard_map(
        body,
        mesh=mesh,
        in_specs=(
            P("grp", "seq", "vocab"),
            P("grp", None, ("vocab", "seq")),
            P(None, ("vocab", "seq")),
            P("seq"),
        ),
        out_specs=(P("grp", "seq", "vocab"), P()),
        check_vma=False,
    )
```

profile of v0, /device:TPU:32, one launch (start us, length us, event | category | flops | bytes accessed | tf_op | source)
XLA Modules:
  0.0 1301.5 jit_solution(1055204296581457326)
XLA Ops:
  7.2 0.0 all-gather.2.cloned.1.call-start
  7.2 0.7 broadcast_select_fusion.5
  7.9 0.8 fusion.14
  8.7 13.1 %all_gather.6 = bf16[256,256]{1,0:T(8,128)(2,1)} all-gather(bf16[64,256]{1,0:T(8,128)(2,1)S(1)} %fusion.14), channel_id=1, replica_groups=mesh['grp'=2,'vocab'=32,'seq'=4] {'seq'}, dimensions={0}, use_global_device_ids=true | all-gather | bytes 163840 | tf_op jit(solution)/shard_map/all_gather | solution.py:29
  21.8 0.0 all-gather.2.cloned.1.call-update
  21.8 0.0 reduce-scatter.3.cloned.1.call-start
  21.9 0.9 broadcast_select_fusion.4
  22.8 10.5 fusion
  33.3 52.6 %all-gather.2.cloned.1.call-done = bf16[256,8192]{1,0:T(8,128)(2,1)} async-done(((bf16[256,256]{1,0:T(8,128)(2,1)}), bf16[256,8192]{1,0:T(8,128)(2,1)}) %all-gather.2.cloned.1.call-update) | async-done | bytes 4194320 | tf_op jit(solution)/shard_map/all_gather | solution.py:31
  85.9 8.4 fusion.16
  94.3 348.4 %pmax.7 = f32[256]{0:T(256)S(1)} all-reduce(f32[256]{0:T(256)S(1)} %get-tuple-element.2), channel_id=1, replica_groups=mesh['grp'=2,'vocab'=32,'seq'=4] {'vocab','seq'}, use_global_device_ids=true, to_apply=%region_1.2 | all-reduce | flops 256 | bytes 2048 | tf_op jit(solution)/shard_map/pmax | solution.py:35
  442.6 0.2 exponential_reduce_fusion
  442.9 343.2 %psum.14 = f32[256]{0:T(256)S(1)} all-reduce(f32[256]{0:T(256)S(1)} %exponential_reduce_fusion), channel_id=1, replica_groups=mesh['grp'=2,'vocab'=32,'seq'=4] {'vocab','seq'}, use_global_device_ids=true, to_apply=%region_3.4 | all-reduce | flops 256 | bytes 2048 | tf_op jit(solution)/shard_map/psum | solution.py:36
  786.1 0.1 subtract_convert_fusion
  786.2 3.5 collective-permute-start
  789.7 5.1 collective-permute-done
  794.8 0.4 fusion.8
  795.2 345.3 %psum.15 = f32[256]{0:T(256)S(1)} all-reduce(f32[256]{0:T(256)S(1)} %fusion.8), channel_id=1, replica_groups=mesh['grp'=2,'vocab'=32,'seq'=4] {'vocab','seq'}, use_global_device_ids=true, to_apply=%region_5.6 | all-reduce | flops 256 | bytes 2048 | tf_op jit(solution)/shard_map/psum | solution.py:44
  1140.5 0.0 copy-start
  1140.5 13.0 fusion.9
  1153.5 0.0 copy-done
  1153.5 0.0 reduce-scatter.3.cloned.1.call-update
  1153.5 0.0 reduce-scatter.5.cloned.1.call-start
  1153.5 115.5 %reduce-scatter.3.cloned.1.call-done = f32[256,256]{1,0:T(8,128)} async-done(((f32[256,8192]{1,0:T(8,128)}), f32[256,256]{1,0:T(8,128)}) %reduce-scatter.3.cloned.1.call-update) | async-done | bytes 262160 | tf_op jit(solution)/shard_map/reduce_scatter | solution.py:51
  1269.0 0.0 reduce-scatter.5.cloned.1.call-update
  1269.0 24.4 %reduce-scatter.5.cloned.1.call-done = f32[64,256]{1,0:T(8,128)} async-done(((f32[256,256]{1,0:T(8,128)}), f32[64,256]{1,0:T(8,128)}) %reduce-scatter.5.cloned.1.call-update) | async-done | bytes 65552 | tf_op jit(solution)/shard_map/reduce_scatter | solution.py:52
  1293.5 1.5 convert_bitcast_fusion
  (1 shorter events, 0.0 us)
Async XLA Ops:
  7.2 78.7 %all-gather.2.cloned.1.call-start = ((), (), s32[]{:S(2)}) async-start(), calls=%async_computation.2 | async-start | bytes 4325376 | tf_op jit(solution)/shard_map/all_gather | solution.py:31
  21.8 1247.2 %reduce-scatter.3.cloned.1.call-start = ((), (), s32[]{:S(2)}) async-start(), calls=%async_computation.3 | async-start | bytes 8650752 | tf_op jit(solution)/shard_map/reduce_scatter | solution.py:51
  786.2 8.6 collective-permute-start
  1140.5 13.0 copy-start
  1153.5 140.0 %reduce-scatter.5.cloned.1.call-start = ((), (), s32[]{:S(2)}) async-start(), calls=%async_computation.4 | async-start | bytes 327680 | tf_op jit(solution)/shard_map/reduce_scatter | solution.py:52
Sparse Core Ops, SparseCore 0:
  21.9 63.8 all-gather.1
  1153.6 115.3 reduce-scatter.2
  1271.7 21.7 reduce-scatter.4
where the time goes:
time: 1300 us
  blocking collectives  1050 us (81%)
  waiting for transfers between devices  198 us (15%)
  matrix products  21.4 us (2%)
  other arithmetic  15.1 us (1%)
  between operations  13.8 us (1%)
    pmax x1, blocking collectives, body(): top = lax.pmax(jnp.max(logits, axis=1), ('vocab', 'seq'))  348 us
    psum x1, blocking collectives, body(): token_kl = lax.psum(jnp.sum(p_ref * diff, axis=1), ('vocab', 'seq'))  345 us
    psum x1, blocking collectives, body(): lax.psum(jnp.sum(jnp.exp(logits - top[:, None]), axis=1), ('vocab', 'seq'))  343 us
    reduce_scatter x1, waiting for transfers between devices, body(): lax.psum_scatter(partial_value, 'vocab', scatter_dimension=1, tiled=True)  115 us
    all_gather x1, waiting for transfers between devices, body(): lax.all_gather(rows, 'vocab', axis=1, tiled=True)  52.6 us
  transfers between devices with their start and end apart: 4, of which 4 were waited for; matrix products, arithmetic and copies ran while one was open for 1% of the time, Pallas kernels for 0%

commit v1 on v0

v1 whole, which is shorter than its diff:
```python
import functools

import jax
import jax.numpy as jnp
from jax import lax
from jax.experimental import pallas as pl
from jax.experimental.pallas import tpu as pltpu
from jax.sharding import Mesh, PartitionSpec as P

loss_scale = 1024.0
MIB = 1024 * 1024
f32 = jnp.float32
bf16 = jnp.bfloat16

AXES = ("g", "zh", "y", "c", "x")
SIZES = (2, 4, 4, 2, 4)
GROUP = 128


def from_shift(value, axis, shift):
    n = lax.axis_size(axis)
    return lax.ppermute(value, axis, [((i + shift) % n, i) for i in range(n)])


def params(mib):
    return pltpu.CompilerParams(vmem_limit_bytes=mib * MIB)


def dequantize_kernel(place, codes, scales, out):
    core, quantized = place[1], place[2]
    for other in range(2):
        source = lax.rem(core + other, 2)
        block = codes[0, 0, source].astype(f32)
        factor = scales[0, 0, source]
        factor = jnp.where(quantized == 1, factor, 1.0)
        half = GROUP
        out[other, 0, 0, :half] = (block[:half] * factor[0:1]).astype(bf16)
        out[other, 0, 0, half:] = (block[half:] * factor[1:2]).astype(bf16)


def dequantize(place, codes, scales):
    zs, ys, cs, feats, cols = codes.shape
    return pl.pallas_call(
        dequantize_kernel,
        grid_spec=pltpu.PrefetchScalarGridSpec(
            num_scalar_prefetch=1,
            grid=(zs, ys),
            in_specs=[
                pl.BlockSpec(
                    (1, 1, cs, feats, cols),
                    lambda z, y, place: (lax.rem(z + place[0], zs), y, 0, 0, 0),
                ),
                pl.BlockSpec(
                    (1, 1, cs, feats // GROUP, cols),
                    lambda z, y, place: (lax.rem(z + place[0], zs), y, 0, 0, 0),
                ),
            ],
            out_specs=pl.BlockSpec(
                (cs, 1, 1, feats, cols), lambda z, y, place: (0, y, z, 0, 0)
            ),
        ),
        out_shape=jax.ShapeDtypeStruct((cs, ys, zs, feats, cols), bf16),
        compiler_params=params(24),
        cost_estimate=pl.CostEstimate(
            flops=zs * ys * cs * feats * cols,
            bytes_accessed=4 * zs * ys * cs * feats * cols,
            transcendentals=0,
        ),
        name="dequantize",
    )(place, codes, scales)


def first_logits_kernel(rows, weights, total):
    step = pl.program_id(0)
    part = jnp.dot(rows[0], weights[0, 0], preferred_element_type=f32)

    @pl.when(step == 0)
    def _():
        total[...] = part

    @pl.when(step > 0)
    def _():
        total[...] += part


def second_logits_kernel(rows, weights, before, total, sent):
    step = pl.program_id(0)
    part = jnp.dot(rows[0], weights[0, 0], preferred_element_type=f32)

    @pl.when(step == 0)
    def _():
        total[...] = before[...] + part

    @pl.when(step > 0)
    def _():
        total[...] += part

    @pl.when(step == pl.num_programs(0) - 1)
    def _():
        logits = total[...]
        cols = logits.shape[1]
        top = jnp.max(logits, axis=1, keepdims=True).astype(bf16)
        sent[:, :cols] = (logits - top.astype(f32)).astype(bf16)
        sent[:, cols:] = jnp.broadcast_to(top, (logits.shape[0], sent.shape[1] - cols))


def logits_part(rows, weights, half, before=None):
    ys, tokens, depth = rows.shape
    cols = weights.shape[-1]
    in_specs = [
        pl.BlockSpec((1, tokens, depth), lambda y: (y, 0, 0)),
        pl.BlockSpec((1, 1, depth, cols), lambda y: (half, y, 0, 0)),
    ]
    total_spec = pl.BlockSpec((tokens, cols), lambda y: (0, 0))
    total_shape = jax.ShapeDtypeStruct((tokens, cols), f32)
    cost = pl.CostEstimate(
        flops=2 * ys * tokens * depth * cols,
        bytes_accessed=2 * ys * depth * (cols + tokens),
        transcendentals=0,
    )
    if before is None:
        return pl.pallas_call(
            first_logits_kernel,
            grid=(ys,),
            in_specs=in_specs,
            out_specs=total_spec,
            out_shape=total_shape,
            compiler_params=params(24),
            cost_estimate=cost,
            name="logits_own",
        )(rows, weights)
    sent = (tokens, cols + 128)
    return pl.pallas_call(
        second_logits_kernel,
        grid=(ys,),
        in_specs=in_specs + [total_spec],
        out_specs=[total_spec, pl.BlockSpec(sent, lambda y: (0, 0))],
        out_shape=[total_shape, jax.ShapeDtypeStruct(sent, bf16)],
        compiler_params=params(24),
        cost_estimate=cost,
        name="logits_other",
    )(rows, weights, before)


def both_logits(quantized, own, received):
    cols = own.shape[1]
    other = received[:, :cols].astype(f32) + received[:, cols : cols + 1].astype(f32)
    return jnp.where(quantized, other, own), jnp.where(quantized, own, other)


def column_to_rows(column):
    tokens = column.shape[0]
    return jnp.transpose(jnp.broadcast_to(column, (tokens, 128)))[0:1, :]


def local_stats_kernel(place, own, received, out):
    quantized = place[2] == 1
    ref, quant = both_logits(quantized, own[...], received[...])
    ref_top = jnp.max(ref, axis=1, keepdims=True)
    ref_exp = jnp.exp(ref - ref_top)
    ref_sum = jnp.sum(ref_exp, axis=1, keepdims=True)
    ref_lse = ref_top + jnp.log(ref_sum)
    mean_diff = jnp.sum(ref_exp * (ref - quant), axis=1, keepdims=True) / ref_sum
    quant_top = jnp.max(quant, axis=1, keepdims=True)
    quant_lse = quant_top + jnp.log(
        jnp.sum(jnp.exp(quant - quant_top), axis=1, keepdims=True)
    )
    first = column_to_rows(ref_lse)
    second = column_to_rows(jnp.where(quantized, quant_lse, mean_diff))
    for i in range(first.shape[1] // 128):
        out[i : i + 1, :] = first[:, i * 128 : i * 128 + 128]
        out[2 + i : 3 + i, :] = second[:, i * 128 : i * 128 + 128]


def local_stats(place, own, received):
    return pl.pallas_call(
        local_stats_kernel,
        in_specs=[
            pl.BlockSpec(memory_space=pltpu.SMEM),
            pl.BlockSpec(memory_space=pltpu.VMEM),
            pl.BlockSpec(memory_space=pltpu.VMEM),
        ],
        out_specs=pl.BlockSpec(memory_space=pltpu.VMEM),
        out_shape=jax.ShapeDtypeStruct((4, 128), f32),
        compiler_params=params(16),
        name="local_stats",
    )(place, own, received)


def rows_to_column(row):
    return jnp.transpose(jnp.broadcast_to(row, (128, row.shape[1])))[:, 0:1]


def gradient(place, own, received, stats):
    quantized = place[2] == 1
    first = jnp.concatenate([stats[:, 0, :], stats[:, 1, :]], axis=1)
    second = jnp.concatenate([stats[:, 2, :], stats[:, 3, :]], axis=1)
    first_top = jnp.max(first, axis=0, keepdims=True)
    first_exp = jnp.exp(first - first_top)
    first_sum = jnp.sum(first_exp, axis=0, keepdims=True)
    ref_lse = first_top + jnp.log(first_sum)
    mean_diff = jnp.sum(first_exp * jnp.where(quantized, 0.0, second), axis=0, keepdims=True) / first_sum
    second_top = jnp.max(second, axis=0, keepdims=True)
    quant_lse = second_top + jnp.log(
        jnp.sum(jnp.exp(second - second_top), axis=0, keepdims=True)
    )
    kl_part = jnp.where(quantized, quant_lse, mean_diff - ref_lse)
    ref, quant = both_logits(quantized, own[...], received[...])
    p_ref = jnp.exp(ref - rows_to_column(ref_lse))
    column = rows_to_column(jnp.where(quantized, quant_lse, mean_diff))
    p_quant = jnp.exp(jnp.where(quantized, quant - column, 0.0))
    grad_ref = p_ref * (ref - quant - column)
    grad = loss_scale * jnp.where(quantized, p_quant - p_ref, grad_ref)
    return grad.astype(bf16), kl_part


def products(grad, weights, out):
    out[0] = lax.dot_general(
        grad, weights[0, 0], (((1,), (1,)), ((), ())), preferred_element_type=f32
    ).astype(bf16)


def first_products_kernel(place, own, received, stats, weights, out, grad, kl_part):
    @pl.when(pl.program_id(0) == 0)
    def _():
        grad_value, kl_value = gradient(place, own, received, stats[...])
        grad[...] = grad_value
        kl_part[...] = kl_value

    products(grad[...], weights, out)


def second_products_kernel(grad, weights, out):
    products(grad[...], weights, out)


def products_part(weights, half, grad=None, sources=None):
    halves, ys, depth, cols = weights.shape
    tokens = 256
    weight_spec = pl.BlockSpec((1, 1, depth, cols), lambda y: (half, y, 0, 0))
    out_spec = pl.BlockSpec((1, tokens, depth), lambda y: (y, 0, 0))
    out_shape = jax.ShapeDtypeStruct((ys, tokens, depth), bf16)
    grad_spec = pl.BlockSpec((tokens, cols), lambda y: (0, 0))
    cost = pl.CostEstimate(
        flops=2 * ys * tokens * depth * cols,
        bytes_accessed=2 * ys * depth * (cols + tokens),
        transcendentals=0,
    )
    if grad is not None:
        return pl.pallas_call(
            second_products_kernel,
            grid=(ys,),
            in_specs=[grad_spec, weight_spec],
            out_specs=out_spec,
            out_shape=out_shape,
            compiler_params=params(24),
            cost_estimate=cost,
            name="products_own",
        )(grad, weights)
    place, own, received, stats = sources
    whole = lambda a: pl.BlockSpec(a.shape, lambda y, n=a.ndim: (0,) * n)
    return pl.pallas_call(
        first_products_kernel,
        grid=(ys,),
        in_specs=[pl.BlockSpec(memory_space=pltpu.SMEM)]
        + [whole(own), whole(received), whole(stats), weight_spec],
        out_specs=[out_spec, grad_spec, pl.BlockSpec((1, tokens), lambda y: (0, 0))],
        out_shape=[
            out_shape,
            jax.ShapeDtypeStruct((tokens, cols), bf16),
            jax.ShapeDtypeStruct((1, tokens), f32),
        ],
        compiler_params=params(24),
        cost_estimate=cost,
        name="products_other",
    )(place, own, received, stats, weights)


def body(hidden_states, head_weights, weight_scales, token_scales):
    zs, ys, cs, xs = (lax.axis_size(a) for a in ("zh", "y", "c", "x"))
    quantized = lax.axis_index("g") == 1
    zh = lax.axis_index("zh")
    place = jnp.stack(
        [zh, lax.axis_index("c"), lax.axis_index("g")]
    ).astype(jnp.int32)
    _, local_tokens, feats = hidden_states.shape
    tokens = local_tokens * xs
    cols = head_weights.shape[2]
    row_factor = jnp.where(quantized, token_scales, 1.0)
    local_rows = (hidden_states[0].astype(f32) * row_factor[:, None]).astype(bf16)

    gathered = jnp.concatenate(
        [local_rows] + [from_shift(local_rows, "zh", k) for k in range(1, zs)], axis=1
    )
    weights = dequantize(
        place,
        head_weights.reshape(zs, ys, cs, feats, cols),
        weight_scales.reshape(zs, ys, cs, feats // GROUP, cols),
    ).reshape(cs, ys, zs * feats, cols)
    own_rows = lax.all_to_all(
        jnp.broadcast_to(gathered[None], (ys * xs,) + gathered.shape),
        ("y", "x"), 0, 0, tiled=True,
    ).reshape(ys, tokens, zs * feats)
    other_rows = from_shift(own_rows, "c", 1)
    logits = logits_part(own_rows, weights, 0)
    logits, sent = logits_part(other_rows, weights, 1, logits)
    received = from_shift(sent, "g", 1)

    stats = local_stats(place, logits, received)
    devices = zs * ys * cs * xs
    stats = lax.all_to_all(
        jnp.broadcast_to(stats[None], (devices,) + stats.shape),
        ("zh", "y", "c", "x"), 0, 0, tiled=True,
    )
    for_other, grad, kl_part = products_part(
        weights, 1, sources=(place, logits, received, stats)
    )
    token_kl = (kl_part + from_shift(kl_part, "g", 1)).reshape(tokens)
    from_other = from_shift(for_other, "c", 1)
    kept = products_part(weights, 0, grad=grad)
    chip = (kept.astype(f32) + from_other.astype(f32)).astype(bf16)
    parts = lax.all_to_all(
        chip.reshape(ys * xs, local_tokens, zs * feats), ("y", "x"), 0, 0, tiled=True
    )
    plane = jnp.sum(parts.astype(f32), axis=0).astype(bf16)
    blocks = plane.reshape(local_tokens, zs, feats).transpose(1, 0, 2)
    blocks = lax.dynamic_slice_in_dim(
        jnp.concatenate([blocks, blocks]), lax.rem(zs - zh, zs), zs, 0
    )
    blocks = lax.all_to_all(blocks, "zh", 0, 0, tiled=True)
    result = jnp.sum(blocks.astype(f32), axis=0).astype(bf16)
    return (result[None], token_kl)


def solution(mesh):
    fine = Mesh(mesh.devices.reshape(SIZES), AXES)
    vocab = ("zh", "y", "c")
    columns = vocab + ("x",)
    return jax.shard_map(
        body,
        mesh=fine,
        in_specs=(P("g", "x", vocab), P("g", None, columns), P(None, columns), P("x")),
        out_specs=(P("g", "x", vocab), P()),
        check_vma=False,
    )
```

time: 1300 us -> 163 us (0.13)
  blocking collectives: 1050 us -> 57.8 us
  waiting for transfers between devices: 198 us -> 55.4 us
  matrix products: 21.4 us -> 0 us
  Pallas kernels: 0 us -> 17.8 us
  starting transfers between devices: 3.63 us -> 19.5 us
  between operations: 13.8 us -> 0.77 us
    psum x2 -> x0, blocking collectives: 689 us -> none  [the longest x1 345 us: body(): token_kl = lax.psum(jnp.sum(p_ref * diff, axis=1), ('vocab', 'seq'))]
    pmax x1 -> x0, blocking collectives: 348 us -> none  [body(): top = lax.pmax(jnp.max(logits, axis=1), ('vocab', 'seq'))]
    reduce_scatter x2 -> x0, waiting for transfers between devices: 140 us -> none  [the longest x1 115 us: body(): lax.psum_scatter(partial_value, 'vocab', scatter_dimension=1, tiled=True)]
    all_to_all x0 -> x2, blocking collectives: none -> 57.8 us  [the longest x1 34.8 us: body(): lax.all_to_all(jnp.broadcast_to(gathered[None], (ys * xs,) + gathered.sha...]
    all_gather x1 -> x0, waiting for transfers between devices: 52.6 us -> none  [body(): lax.all_gather(rows, 'vocab', axis=1, tiled=True)]
    all_to_all x0 -> x2, waiting for transfers between devices: none -> 38 us  [the longest x1 33.9 us: body(): lax.all_to_all(chip.reshape(ys * xs, local_tokens, zs * feats), ('y', 'x'...]
    dot_general x2 -> x0, matrix products: 21.4 us -> none  [the longest x1 13 us: body(): lax.dot_general(grad_logits, weights, (((1,), (1,)), ((), ())), preferred...]
    pallas_call x0 -> x6, Pallas kernels: none -> 17.8 us  [the longest x1 4.22 us: logits_part(): pl.pallas_call(second_logits_kernel, grid=(ys,), in_specs=in_specs + [tot...]
  transfers between devices with their start and end apart: 4 -> 9, of which waited for: 4 -> 7; matrix products, arithmetic and copies ran while one was open for 1% -> 0% of each run, Pallas kernels for 0% -> 5%
where the time goes in v1:
time: 163 us; the launch traced here: 162 us
  blocking collectives  57.8 us (35%)
  waiting for transfers between devices  55.4 us (34%)
  starting transfers between devices  19.5 us (12%)
  Pallas kernels  17.8 us (11%)
  other arithmetic  5.77 us (4%)
  local copies, waits for them, and re-layouts  5.13 us (3%)
    all_to_all x1, blocking collectives, body(): lax.all_to_all(jnp.broadcast_to(gathered[None], (ys * xs,) + gathered.sha...  34.8 us
    all_to_all x1, waiting for transfers between devices, body(): lax.all_to_all(chip.reshape(ys * xs, local_tokens, zs * feats), ('y', 'x'...  33.9 us
    all_to_all x1, blocking collectives, body(): lax.all_to_all(jnp.broadcast_to(stats[None], (devices,) + stats.shape), (...  22.9 us
    ppermute x7, waiting for transfers between devices, from_shift(): return lax.ppermute(value, axis, [((i + shift) % n, i) for i in range(n)])  17.3 us
    ppermute x7, starting transfers between devices, from_shift(): return lax.ppermute(value, axis, [((i + shift) % n, i) for i in range(n)])  12.4 us
    pallas_call x1, Pallas kernels, logits_part(): pl.pallas_call(second_logits_kernel, grid=(ys,), in_specs=in_specs + [tot...  4.22 us
    all_to_all x1, waiting for transfers between devices, body(): blocks = lax.all_to_all(blocks, 'zh', 0, 0, tiled=True)  4.13 us
    unnamed x4, local copies, waits for them, and re-layouts  4.01 us
  transfers between devices with their start and end apart: 9, of which 7 were waited for; matrix products, arithmetic and copies ran while one was open for 0% of the time, Pallas kernels for 5%

profile of v1, /device:TPU:32, one launch (start us, length us, event | category | flops | bytes accessed | tf_op | source)
XLA Modules:
  0.0 162.1 jit_solution(14329729235713419092)
XLA Ops:
  0.6 0.7 broadcast_select_fusion
  1.3 0.8 fusion.1
  2.1 3.3 %collective-permute-start.2 = (bf16[64,256]{1,0:T(8,128)(2,1)S(1)}, bf16[64,256]{1,0:T(8,128)(2,1)S(1)}, u32[]{:S(2)}, u32[]{:S(2)}) collective-permute-start(bf16[64,256]{1,0:T(8,128)(2,1)S(1)} %fusion.1), channel_id=1, source_target_pairs={{96,0},{0,32},{32,64},{64,96},{97,1},{1,33},{33,65},{65,97},{98,2}... | collective-permute-start | bytes 98312 | tf_op jit(solution)/shard_map/ppermute | solution.py:22
  5.5 4.5 %collective-permute-start.1 = (bf16[64,256]{1,0:T(8,128)(2,1)S(1)}, bf16[64,256]{1,0:T(8,128)(2,1)S(1)}, u32[]{:S(2)}, u32[]{:S(2)}) collective-permute-start(bf16[64,256]{1,0:T(8,128)(2,1)S(1)} %fusion.1), channel_id=1, source_target_pairs={{64,0},{96,32},{0,64},{32,96},{65,1},{97,33},{1,65},{33,97},{66,2}... | collective-permute-start | bytes 98312 | tf_op jit(solution)/shard_map/ppermute | solution.py:22
  10.0 2.7 %collective-permute-start = (bf16[64,256]{1,0:T(8,128)(2,1)S(1)}, bf16[64,256]{1,0:T(8,128)(2,1)S(1)}, u32[]{:S(2)}, u32[]{:S(2)}) collective-permute-start(bf16[64,256]{1,0:T(8,128)(2,1)S(1)} %fusion.1), channel_id=1, source_target_pairs={{32,0},{64,32},{96,64},{0,96},{33,1},{65,33},{97,65},{1,97},{34,2}... | collective-permute-start | bytes 98312 | tf_op jit(solution)/shard_map/ppermute | solution.py:22
  12.6 0.8 collective-permute-done.1
  13.4 1.4 collective-permute-done
  14.9 0.3 broadcast_in_dim.11
  15.2 34.8 %all_to_all.20 = bf16[16,64,1024]{2,1,0:T(8,128)(2,1)S(1)} all-to-all(bf16[16,64,1024]{2,1,0:T(8,128)(2,1)S(1)} %broadcast_in_dim.11), channel_id=1, replica_groups=mesh['g'=2,'zh'=4,'y'=4,'c'=2,'x'=4] {'y','x'}, dimensions={0} | all-to-all | bytes 4194304 | tf_op jit(solution)/shard_map/all_to_all | solution.py:300
  50.2 4.0 %copy-done = bf16[1,8192,640]{2,1,0:T(8,128)(2,1)S(1)} copy-done((bf16[1,8192,640]{2,1,0:T(8,128)(2,1)S(1)}, bf16[1,8192,640]{2,1,0:T(8,128)(2,1)}, u32[]{:S(2)}) %copy-start) | copy-done | bytes 10485784
  54.2 3.6 %dequantize.1 = bf16[2,4,4,256,640]{4,3,2,1,0:T(8,128)(2,1)S(1)} custom-call(s32[3]{0:T(128)S(1)} %pad_add_fusion.place, bf16[4,4,2,256,640]{4,3,2,1,0:T(8,128)(2,1)S(1)} %bitcast.17, f32[4,4,2,2,640]{4,3,2,1,0:T(2,128)S(1)} %reshape.32.scales), custom_call_target="tpu_custom_call" | custom-call | flops 5242880 | bytes 20971520 | tf_op jit(solution)/shard_map/dequantize/pallas_call | solution.py:43
  57.8 2.6 %logits_own.1.before = f32[256,640]{1,0:T(8,128)S(1)} custom-call(bf16[4,256,1024]{2,1,0:T(8,128)(2,1)S(1)} %bitcast.19, bf16[2,4,1024,640]{3,2,1,0:T(8,128)(2,1)S(1)} %bitcast.13), custom_call_target="tpu_custom_call" | custom-call | flops 1342177280 | bytes 7340032 | tf_op jit(solution)/shard_map/logits_own/pallas_call | solution.py:122
  60.4 4.2 %logits_other.1 = (f32[256,640]{1,0:T(8,128)S(1)}, bf16[256,768]{1,0:T(8,128)(2,1)S(1)}) custom-call(bf16[4,256,1024]{2,1,0:T(8,128)(2,1)} %collective-permute-done.3.rows, bf16[2,4,1024,640]{3,2,1,0:T(8,128)(2,1)S(1)} %bitcast.14, f32[256,640]{1,0:T(8,128)S(1)} %logits_own.1.before), custom_call_target="tpu_custom_call" | custom-call | flops 1342177280 | bytes 7340032 | tf_op jit(solution)/shard_map/logits_other/pallas_call | solution.py:133
  64.6 0.8 collective-permute-start.4
  65.5 10.8 %collective-permute-done.4.received = bf16[256,768]{1,0:T(8,128)(2,1)S(1)} collective-permute-done((bf16[256,768]{1,0:T(8,128)(2,1)S(1)}, bf16[256,768]{1,0:T(8,128)(2,1)S(1)}, u32[]{:S(2)}, u32[]{:S(2)}) %collective-permute-start.4) | collective-permute-done | bytes 393248 | tf_op jit(solution)/shard_map/ppermute | solution.py:22
  76.2 1.2 local_stats.1
  77.5 22.9 %all_to_all.21.stats = f32[128,4,128]{2,1,0:T(4,128)S(1)} all-to-all(f32[128,4,128]{2,1,0:T(4,128)S(1)} %broadcast_in_dim.22), channel_id=1, replica_groups=mesh['g'=2,'zh'=4,'y'=4,'c'=2,'x'=4] {'zh','y','c','x'}, dimensions={0} | all-to-all | bytes 524288 | tf_op jit(solution)/shard_map/all_to_all | solution.py:311
  100.4 3.8 %products_other.1 = (bf16[4,256,1024]{2,1,0:T(8,128)(2,1)S(1)}, bf16[256,640]{1,0:T(8,128)(2,1)S(1)}, f32[1,256]{1,0:T(1,128)S(1)}) custom-call(s32[3]{0:T(128)S(1)} %pad_add_fusion.place, f32[256,640]{1,0:T(8,128)S(1)} %get-tuple-element.7.own, bf16[256,768]{1,0:T(8,128)(2,1)S(1)} %collective-permute-done.4.received, f32[128,4,128]{2,1,0:T(4,128)S(1)} %all_to_all.21.stats, ...), custom_call_target="tpu_custom_call" | custom-call | flops 1342177280 | bytes 7340032 | tf_op jit(solution)/shard_map/products_other/pallas_call | solution.py:262
  104.4 2.5 %products_own.1 = bf16[4,256,1024]{2,1,0:T(8,128)(2,1)S(1)} custom-call(bf16[256,640]{1,0:T(8,128)(2,1)S(1)} %get-tuple-element.9.grad, bf16[2,4,1024,640]{3,2,1,0:T(8,128)(2,1)S(1)} %bitcast.16), custom_call_target="tpu_custom_call" | custom-call | flops 1342177280 | bytes 7340032 | tf_op jit(solution)/shard_map/products_own/pallas_call | solution.py:250
  106.9 1.6 collective-permute-done.5
  108.4 2.3 %add_convert_fusion = bf16[4,256,1024]{2,1,0:T(8,128)(2,1)} fusion(bf16[4,256,1024]{2,1,0:T(8,128)(2,1)S(1)} %collective-permute-done.5, bf16[4,256,1024]{2,1,0:T(8,128)(2,1)S(1)} %products_own.1), kind=kLoop, calls=%fused_computation | loop fusion | flops 4194304 | bytes 6291456 | tf_op jit(solution)/shard_map/convert_element_type | solution.py:321
  110.8 3.7 %all-to-all-start.2 = ((bf16[16,64,1024]{2,1,0:T(8,128)(2,1)}), bf16[16,64,1024]{2,1,0:T(8,128)(2,1)S(1)}, u32[]{:S(2)}, u32[]{:S(2)}) async-start(bf16[16,64,1024]{2,1,0:T(8,128)(2,1)} %bitcast.7), calls=%async_computation.2 | async-start | bytes 4194304 | tf_op jit(solution)/shard_map/all_to_all | solution.py:322
  114.5 33.9 %all-to-all-done.2 = bf16[16,64,1024]{2,1,0:T(8,128)(2,1)S(1)} async-done(((bf16[16,64,1024]{2,1,0:T(8,128)(2,1)}), bf16[16,64,1024]{2,1,0:T(8,128)(2,1)S(1)}, u32[]{:S(2)}, u32[]{:S(2)}) %all-to-all-start.2) | async-done | bytes 2097184 | tf_op jit(solution)/shard_map/all_to_all | solution.py:322
  148.4 0.4 reduce_sum.24
  148.9 0.3 fusion
  149.1 0.7 copy.6
  149.8 3.3 %all-to-all-start.3 = ((bf16[4,64,256]{2,1,0:T(8,128)(2,1)}), bf16[4,64,256]{2,1,0:T(8,128)(2,1)S(1)}, u32[]{:S(2)}, u32[]{:S(2)}) async-start(bf16[4,64,256]{2,1,0:T(8,128)(2,1)} %copy.6), calls=%async_computation.3 | async-start | bytes 262144 | tf_op jit(solution)/shard_map/all_to_all | solution.py:330
  153.1 0.9 collective-permute-start.6
  154.0 2.8 %collective-permute-done.6 = f32[1,256]{1,0:T(1,128)S(1)} collective-permute-done((f32[1,256]{1,0:T(1,128)S(1)}, f32[1,256]{1,0:T(1,128)S(1)}, u32[]{:S(2)}, u32[]{:S(2)}) %collective-permute-start.6) | collective-permute-done | bytes 1056 | tf_op jit(solution)/shard_map/ppermute | solution.py:22
  156.8 0.6 add.11
  157.3 4.1 %all-to-all-done.3 = bf16[4,64,256]{2,1,0:T(8,128)(2,1)S(1)} async-done(((bf16[4,64,256]{2,1,0:T(8,128)(2,1)}), bf16[4,64,256]{2,1,0:T(8,128)(2,1)S(1)}, u32[]{:S(2)}, u32[]{:S(2)}) %all-to-all-start.3) | async-done | bytes 131104 | tf_op jit(solution)/shard_map/all_to_all | solution.py:330
  161.5 0.6 reduce_sum.25
  (12 shorter events, 0.5 us)
Async XLA Ops:
  2.1 10.5 %collective-permute-start.2 = (bf16[64,256]{1,0:T(8,128)(2,1)S(1)}, bf16[64,256]{1,0:T(8,128)(2,1)S(1)}, u32[]{:S(2)}, u32[]{:S(2)}) collective-permute-start(bf16[64,256]{1,0:T(8,128)(2,1)S(1)} %fusion.1), channel_id=1, source_target_pairs={{96,0},{0,32},{32,64},{64,96},{97,1},{1,33},{33,65},{65,97},{98,2}... | collective-permute-start | bytes 98312 | tf_op jit(solution)/shard_map/ppermute | solution.py:22
  5.5 8.0 %collective-permute-start.1 = (bf16[64,256]{1,0:T(8,128)(2,1)S(1)}, bf16[64,256]{1,0:T(8,128)(2,1)S(1)}, u32[]{:S(2)}, u32[]{:S(2)}) collective-permute-start(bf16[64,256]{1,0:T(8,128)(2,1)S(1)} %fusion.1), channel_id=1, source_target_pairs={{64,0},{96,32},{0,64},{32,96},{65,1},{97,33},{1,65},{33,97},{66,2}... | collective-permute-start | bytes 98312 | tf_op jit(solution)/shard_map/ppermute | solution.py:22
  10.0 4.9 %collective-permute-start = (bf16[64,256]{1,0:T(8,128)(2,1)S(1)}, bf16[64,256]{1,0:T(8,128)(2,1)S(1)}, u32[]{:S(2)}, u32[]{:S(2)}) collective-permute-start(bf16[64,256]{1,0:T(8,128)(2,1)S(1)} %fusion.1), channel_id=1, source_target_pairs={{32,0},{64,32},{96,64},{0,96},{33,1},{65,33},{97,65},{1,97},{34,2}... | collective-permute-start | bytes 98312 | tf_op jit(solution)/shard_map/ppermute | solution.py:22
  15.1 34.9 %copy-start.1 = (f32[64,640]{1,0:T(8,128)S(1)}, f32[64,640]{1,0:T(8,128)}, u32[]{:S(2)}) copy-start(f32[64,640]{1,0:T(8,128)} %param.6) | copy-start | bytes 491524
  50.0 10.4 %collective-permute-start.3 = (bf16[4,256,1024]{2,1,0:T(8,128)(2,1)S(1)}, bf16[4,256,1024]{2,1,0:T(8,128)(2,1)}, u32[]{:S(2)}, u32[]{:S(2)}) collective-permute-start(bf16[4,256,1024]{2,1,0:T(8,128)(2,1)S(1)} %bitcast.18), channel_id=1, source_target_pairs={{4,0},{0,4},{5,1},{1,5},{6,2},{2,6},{7,3},{3,7},{12,8},{8,12},{13,... | collective-permute-start | bytes 6291464 | tf_op jit(solution)/shard_map/ppermute | solution.py:22
  50.2 4.0 %copy-start = (bf16[1,8192,640]{2,1,0:T(8,128)(2,1)S(1)}, bf16[1,8192,640]{2,1,0:T(8,128)(2,1)}, u32[]{:S(2)}) copy-start(bf16[1,8192,640]{2,1,0:T(8,128)(2,1)} %param.5) | copy-start | bytes 31457284
  64.6 11.6 %collective-permute-start.4 = (bf16[256,768]{1,0:T(8,128)(2,1)S(1)}, bf16[256,768]{1,0:T(8,128)(2,1)S(1)}, u32[]{:S(2)}, u32[]{:S(2)}) collective-permute-start(bf16[256,768]{1,0:T(8,128)(2,1)S(1)} %get-tuple-element.8), channel_id=1, source_target_pairs={{128,0},{0,128},{129,1},{1,129},{130,2},{2,130},{131,3},{3,131},{1... | collective-permute-start | bytes 1179656 | tf_op jit(solution)/shard_map/ppermute | solution.py:22
  104.2 4.2 %collective-permute-start.5 = (bf16[4,256,1024]{2,1,0:T(8,128)(2,1)S(1)}, bf16[4,256,1024]{2,1,0:T(8,128)(2,1)S(1)}, u32[]{:S(2)}, u32[]{:S(2)}) collective-permute-start(bf16[4,256,1024]{2,1,0:T(8,128)(2,1)S(1)} %get-tuple-element.10), channel_id=1, source_target_pairs={{4,0},{0,4},{5,1},{1,5},{6,2},{2,6},{7,3},{3,7},{12,8},{8,12},{13,... | collective-permute-start | bytes 6291464 | tf_op jit(solution)/shard_map/ppermute | solution.py:22
  110.8 37.6 %all-to-all-start.2 = ((bf16[16,64,1024]{2,1,0:T(8,128)(2,1)}), bf16[16,64,1024]{2,1,0:T(8,128)(2,1)S(1)}, u32[]{:S(2)}, u32[]{:S(2)}) async-start(bf16[16,64,1024]{2,1,0:T(8,128)(2,1)} %bitcast.7), calls=%async_computation.2 | async-start | bytes 4194304 | tf_op jit(solution)/shard_map/all_to_all | solution.py:322
  149.8 11.7 %all-to-all-start.3 = ((bf16[4,64,256]{2,1,0:T(8,128)(2,1)}), bf16[4,64,256]{2,1,0:T(8,128)(2,1)S(1)}, u32[]{:S(2)}, u32[]{:S(2)}) async-start(bf16[4,64,256]{2,1,0:T(8,128)(2,1)} %copy.6), calls=%async_computation.3 | async-start | bytes 262144 | tf_op jit(solution)/shard_map/all_to_all | solution.py:330
  153.1 3.7 %collective-permute-start.6 = (f32[1,256]{1,0:T(1,128)S(1)}, f32[1,256]{1,0:T(1,128)S(1)}, u32[]{:S(2)}, u32[]{:S(2)}) collective-permute-start(f32[1,256]{1,0:T(1,128)S(1)} %get-tuple-element.11), channel_id=1, source_target_pairs={{128,0},{0,128},{129,1},{1,129},{130,2},{2,130},{131,3},{3,131},{1... | collective-permute-start | bytes 3080 | tf_op jit(solution)/shard_map/ppermute | solution.py:22

commit v2 on v1

v2 whole, which is shorter than its diff:
```python
import functools

import jax
import jax.numpy as jnp
from jax import lax
from jax.experimental import pallas as pl
from jax.experimental.pallas import tpu as pltpu
from jax.sharding import Mesh, PartitionSpec as P

loss_scale = 1024.0
MIB = 1024 * 1024
GROUP = 128
f32 = jnp.float32
bf16 = jnp.bfloat16

AXES = ("g", "zh", "y", "c", "x")
SIZES = (2, 4, 4, 2, 4)


def from_shift(value, axis, shift):
    n = lax.axis_size(axis)
    return lax.ppermute(value, axis, [((i + shift) % n, i) for i in range(n)])


def gather_ring(value, axis, zero):
    following = from_shift(value, axis, 1)
    previous = from_shift(value, axis, 3)
    half = value.shape[0] // 2
    opposite = (
        from_shift(following[:half] + zero, axis, 1),
        from_shift(previous[half:] + zero, axis, 3),
    )
    return value, following, previous, opposite


def total(*parts):
    return sum(part.astype(f32) for part in parts).astype(bf16)


def params(mib):
    return pltpu.CompilerParams(vmem_limit_bytes=mib * MIB)


def pick(step, values):
    value = jnp.int32(values[0])
    for i, other in enumerate(values[1:], 1):
        value = jnp.where(step == i, jnp.int32(other), value)
    return value


def dequantize_kernel(place, codes, scales, out, ready):
    core, quantized = place[1], place[2]
    for other in range(2):
        source = lax.rem(core + other, 2)
        block = codes[0, 0, source].astype(f32)
        factor = scales[0, 0, source]
        factor = jnp.where(quantized == 1, factor, 1.0)
        half = GROUP
        out[other, 0, 0, :half] = (block[:half] * factor[0:1]).astype(bf16)
        out[other, 0, 0, half:] = (block[half:] * factor[1:2]).astype(bf16)
    ready[...] = jnp.zeros(ready.shape, ready.dtype)


def dequantize(place, codes, scales):
    zs, ys, cs, feats, cols = codes.shape
    where = lambda z, y, place: (z, lax.rem(y + place[0], ys), 0, 0, 0)
    return pl.pallas_call(
        dequantize_kernel,
        grid_spec=pltpu.PrefetchScalarGridSpec(
            num_scalar_prefetch=1,
            grid=(zs, ys),
            in_specs=[
                pl.BlockSpec((1, 1, cs, feats, cols), where),
                pl.BlockSpec((1, 1, cs, feats // GROUP, cols), where),
            ],
            out_specs=[
                pl.BlockSpec((cs, 1, 1, feats, cols), lambda z, y, place: (0, y, z, 0, 0)),
                pl.BlockSpec((16, 128), lambda z, y, place: (0, 0)),
            ],
        ),
        out_shape=[
            jax.ShapeDtypeStruct((cs, ys, zs, feats, cols), bf16),
            jax.ShapeDtypeStruct((16, 128), bf16),
        ],
        compiler_params=params(24),
        cost_estimate=pl.CostEstimate(
            flops=zs * ys * cs * feats * cols,
            bytes_accessed=4 * zs * ys * cs * feats * cols,
            transcendentals=0,
        ),
        name="dequantize",
    )(place, codes, scales)


def column_to_row(column):
    tokens = column.shape[0]
    return jnp.transpose(jnp.broadcast_to(column, (tokens, 128)))[0:1, :]


def row_to_column(row):
    return jnp.transpose(jnp.broadcast_to(row, (128, row.shape[1])))[:, 0:1]


def logits_kernel(counts, resumed, last, *refs):
    rows, refs = refs[: sum(counts)], refs[sum(counts) :]
    weights, refs = refs[0], refs[1:]
    if resumed:
        before, refs = refs[0], refs[1:]
    logits, refs = refs[0], refs[1:]
    step = pl.program_id(0)
    start = 0
    for i, count in enumerate(counts):
        parts = rows[start : start + count]
        start += count

        @pl.when(step == i)
        def _(i=i, parts=parts):
            block = jnp.concatenate([part[...] for part in parts], axis=0)
            value = jnp.dot(block, weights[0, 0], preferred_element_type=f32)
            if i:
                value = logits[...] + value
            elif resumed:
                value = before[...] + value
            logits[...] = value
            if last and i == len(counts) - 1:
                sent = refs[0]
                tokens, cols = value.shape
                top = jnp.max(value, axis=1, keepdims=True).astype(bf16).astype(f32)
                sent[:tokens] = (value - top).astype(bf16)
                extra = sent.shape[0] - tokens
                row = jnp.broadcast_to(column_to_row(top), (extra, tokens))
                sent[tokens:, :tokens] = row.astype(bf16)
                sent[tokens:, tokens:] = jnp.zeros((extra, cols - tokens), bf16)


def logits_part(blocks, weights, before=None, last=False):
    _, _, depth, cols = weights.shape
    tokens = sum(part.shape[0] for part in blocks[0][2])
    halves = [half for half, _, _ in blocks]
    places = [place for _, place, _ in blocks]
    rows = [part for _, _, parts in blocks for part in parts]
    whole = lambda shape: pl.BlockSpec(shape, lambda s: (0, 0))
    in_specs = [whole(part.shape) for part in rows] + [
        pl.BlockSpec((1, 1, depth, cols), lambda s: (pick(s, halves), pick(s, places), 0, 0))
    ]
    operands = rows + [weights]
    if before is not None:
        in_specs.append(whole((tokens, cols)))
        operands.append(before)
    out_specs = [whole((tokens, cols))]
    out_shape = [jax.ShapeDtypeStruct((tokens, cols), f32)]
    if last:
        out_specs.append(whole((tokens + 16, cols)))
        out_shape.append(jax.ShapeDtypeStruct((tokens + 16, cols), bf16))
    counts = [len(parts) for _, _, parts in blocks]
    return pl.pallas_call(
        functools.partial(logits_kernel, counts, before is not None, last),
        grid=(len(blocks),),
        in_specs=in_specs,
        out_specs=out_specs,
        out_shape=out_shape,
        compiler_params=params(24),
        cost_estimate=pl.CostEstimate(
            flops=2 * len(blocks) * tokens * depth * cols,
            bytes_accessed=2 * len(blocks) * depth * (cols + tokens),
            transcendentals=0,
        ),
        name="logits",
    )(*operands)


def both_logits(quantized, own, received):
    tokens = own.shape[0]
    top = row_to_column(received[tokens : tokens + 1, :tokens].astype(f32))
    other = received[:tokens, :].astype(f32) + top
    return jnp.where(quantized, other, own), jnp.where(quantized, own, other)


def local_stats_kernel(place, own, received, out):
    quantized = place[2] == 1
    ref, quant = both_logits(quantized, own[...], received[...])
    ref_top = jnp.max(ref, axis=1, keepdims=True)
    ref_exp = jnp.exp(ref - ref_top)
    ref_sum = jnp.sum(ref_exp, axis=1, keepdims=True)
    ref_lse = ref_top + jnp.log(ref_sum)
    mean_diff = jnp.sum(ref_exp * (ref - quant), axis=1, keepdims=True) / ref_sum
    quant_top = jnp.max(quant, axis=1, keepdims=True)
    quant_lse = quant_top + jnp.log(
        jnp.sum(jnp.exp(quant - quant_top), axis=1, keepdims=True)
    )
    first = column_to_row(ref_lse)
    second = column_to_row(jnp.where(quantized, quant_lse, mean_diff))
    for i in range(first.shape[1] // 128):
        out[i : i + 1, :] = first[:, i * 128 : i * 128 + 128]
        out[2 + i : 3 + i, :] = second[:, i * 128 : i * 128 + 128]


def local_stats(place, own, received):
    return pl.pallas_call(
        local_stats_kernel,
        in_specs=[
            pl.BlockSpec(memory_space=pltpu.SMEM),
            pl.BlockSpec(memory_space=pltpu.VMEM),
            pl.BlockSpec(memory_space=pltpu.VMEM),
        ],
        out_specs=pl.BlockSpec(memory_space=pltpu.VMEM),
        out_shape=jax.ShapeDtypeStruct((4, 128), f32),
        compiler_params=params(16),
        name="local_stats",
    )(place, own, received)


def gradient(place, own, received, stats):
    quantized = place[2] == 1
    first = jnp.concatenate([stats[:, 0, :], stats[:, 1, :]], axis=1)
    second = jnp.concatenate([stats[:, 2, :], stats[:, 3, :]], axis=1)
    first_top = jnp.max(first, axis=0, keepdims=True)
    first_exp = jnp.exp(first - first_top)
    first_sum = jnp.sum(first_exp, axis=0, keepdims=True)
    ref_lse = first_top + jnp.log(first_sum)
    mean_diff = (
        jnp.sum(first_exp * jnp.where(quantized, 0.0, second), axis=0, keepdims=True)
        / first_sum
    )
    second_top = jnp.max(second, axis=0, keepdims=True)
    quant_lse = second_top + jnp.log(
        jnp.sum(jnp.exp(second - second_top), axis=0, keepdims=True)
    )
    kl_part = jnp.where(quantized, quant_lse, mean_diff - ref_lse)
    ref, quant = both_logits(quantized, own[...], received[...])
    p_ref = jnp.exp(ref - row_to_column(ref_lse))
    column = row_to_column(jnp.where(quantized, quant_lse, mean_diff))
    p_quant = jnp.exp(jnp.where(quantized, quant - column, 0.0))
    grad_ref = p_ref * (ref - quant - column)
    grad = loss_scale * jnp.where(quantized, p_quant - p_ref, grad_ref)
    return grad.astype(bf16), kl_part


def products(grad, weights, outs):
    value = lax.dot_general(
        grad, weights[0, 0], (((1,), (1,)), ((), ())), preferred_element_type=f32
    ).astype(bf16)
    for i, out in enumerate(outs):

        @pl.when(pl.program_id(0) == i)
        def _(out=out):
            out[...] = value


def first_products_kernel(place, own, received, stats, weights, *outs):
    *outs, grad, kl_part = outs

    @pl.when(pl.program_id(0) == 0)
    def _():
        grad_value, kl_value = gradient(place, own, received, stats[...])
        grad[...] = grad_value
        kl_part[...] = kl_value

    products(grad[...], weights, outs)


def more_products_kernel(grad, weights, *outs):
    products(grad[...], weights, outs)


def products_part(blocks, weights, tokens, grad=None, sources=None):
    _, _, depth, cols = weights.shape
    halves = [half for half, _ in blocks]
    places = [place for _, place in blocks]
    whole = lambda shape: pl.BlockSpec(shape, lambda s, n=len(shape): (0,) * n)
    weight_spec = pl.BlockSpec(
        (1, 1, depth, cols), lambda s: (pick(s, halves), pick(s, places), 0, 0)
    )
    out_specs = [whole((tokens, depth))] * len(blocks)
    out_shape = [jax.ShapeDtypeStruct((tokens, depth), bf16)] * len(blocks)
    cost = pl.CostEstimate(
        flops=2 * len(blocks) * tokens * depth * cols,
        bytes_accessed=2 * len(blocks) * depth * (cols + tokens),
        transcendentals=0,
    )
    if grad is not None:
        return pl.pallas_call(
            more_products_kernel,
            grid=(len(blocks),),
            in_specs=[whole(grad.shape), weight_spec],
            out_specs=out_specs,
            out_shape=out_shape,
            compiler_params=params(24),
            cost_estimate=cost,
            name="products",
        )(grad, weights)
    place, own, received, stats = sources
    return pl.pallas_call(
        first_products_kernel,
        grid=(len(blocks),),
        in_specs=[pl.BlockSpec(memory_space=pltpu.SMEM)]
        + [whole(own.shape), whole(received.shape), whole(stats.shape), weight_spec],
        out_specs=out_specs + [whole((tokens, cols)), whole((1, tokens))],
        out_shape=out_shape
        + [
            jax.ShapeDtypeStruct((tokens, cols), bf16),
            jax.ShapeDtypeStruct((1, tokens), f32),
        ],
        compiler_params=params(24),
        cost_estimate=cost,
        name="gradient_products",
    )(place, own, received, stats, weights)


def body(hidden_states, head_weights, weight_scales, token_scales):
    zs, ys, cs, xs = (lax.axis_size(a) for a in ("zh", "y", "c", "x"))
    quantized = lax.axis_index("g") == 1
    _, local_tokens, feats = hidden_states.shape
    tokens = local_tokens * xs
    cols = head_weights.shape[2]
    place = jnp.stack([lax.axis_index(a) for a in ("y", "c", "g")]).astype(jnp.int32)
    row_factor = jnp.where(quantized, token_scales, 1.0)
    local_rows = (hidden_states[0].astype(f32) * row_factor[:, None]).astype(bf16)
    weights, ready = dequantize(
        place,
        head_weights.reshape(zs, ys, cs, feats, cols),
        weight_scales.reshape(zs, ys, cs, feats // GROUP, cols),
    )
    weights = weights.reshape(cs, ys, zs * feats, cols)

    rows = lax.all_to_all(
        jnp.broadcast_to(local_rows[None], (zs * xs,) + local_rows.shape),
        ("zh", "x"), 0, 0, tiled=True,
    ).reshape(zs, tokens, feats)
    rows = jnp.concatenate([rows[z] for z in range(zs)], axis=1)
    own, following, previous, opposite = gather_ring(rows, "y", ready[0, 0])
    near = [(0, (own,)), (1, (following,)), (3, (previous,))]
    across = lambda parts: tuple(from_shift(part, "c", 1) for part in parts)
    logits, = logits_part([(0, p, parts) for p, parts in near], weights)
    logits, = logits_part([(1, p, across(parts)) for p, parts in near], weights, logits)
    opposite, logits = lax.optimization_barrier((opposite, logits))
    logits, sent = logits_part(
        [(0, 2, opposite), (1, 2, across(opposite))], weights, logits, last=True
    )
    received = from_shift(sent, "g", 1)

    stats = local_stats(place, logits, received)
    devices = zs * ys * cs * xs
    stats = lax.all_to_all(
        jnp.broadcast_to(stats[None], (devices,) + stats.shape),
        ("zh", "y", "c", "x"), 0, 0, tiled=True,
    )

    sent_2, kept_2, grad, kl_part = products_part(
        [(1, 2), (0, 2)], weights, tokens, sources=(place, logits, received, stats)
    )
    came_2 = from_shift(sent_2, "c", 1)
    sent_1, sent_3, sent_0 = products_part(
        [(1, 1), (1, 3), (1, 0)], weights, tokens, grad=grad
    )
    opposite = total(kept_2, came_2)
    came_1, came_3, came_0 = (from_shift(a, "c", 1) for a in (sent_1, sent_3, sent_0))
    kept_1, kept_3, kept_0 = products_part(
        [(0, 1), (0, 3), (0, 0)], weights, tokens, grad=grad
    )
    half = tokens // 2
    low = from_shift(opposite[:half], "y", 3)
    high = from_shift(opposite[half:], "y", 1)
    following = jnp.concatenate(
        [total(kept_1[:half], came_1[:half], low), total(kept_1[half:], came_1[half:])]
    )
    previous = jnp.concatenate(
        [total(kept_3[:half], came_3[:half]), total(kept_3[half:], came_3[half:], high)]
    )
    kl_other = from_shift(kl_part, "g", 1)
    own = total(
        kept_0, came_0, from_shift(following, "y", 3), from_shift(previous, "y", 1)
    )
    own, kl_other = lax.optimization_barrier((own, kl_other))
    own = jnp.concatenate([own[:, z * feats : (z + 1) * feats] for z in range(zs)])
    own = lax.all_to_all(
        own.reshape(zs * xs, local_tokens, feats), ("zh", "x"), 0, 0, tiled=True
    )
    own = jnp.sum(own.astype(f32), axis=0).astype(bf16)
    return (own[None], (kl_part + kl_other).reshape(tokens))


def solution(mesh):
    fine = Mesh(mesh.devices.reshape(SIZES), AXES)
    vocab = ("zh", "y", "c")
    columns = vocab + ("x",)
    return jax.shard_map(
        body,
        mesh=fine,
        in_specs=(P("g", "x", vocab), P("g", None, columns), P(None, columns), P("x")),
        out_specs=(P("g", "x", vocab), P()),
        check_vma=False,
    )
```

time: 163 us -> 152 us (0.933)
  blocking collectives: 57.8 us -> 52.1 us
  waiting for transfers between devices: 55.4 us -> 51 us
    all_to_all x2 -> x1, waiting for transfers between devices: 38 us -> 16.8 us  [body(): lax.all_to_all(own.reshape(zs * xs, local_tokens, feats), ('zh', 'x'), 0,...]
    ppermute x7 -> x19, waiting for transfers between devices: 17.3 us -> 34.2 us  [from_shift(): return lax.ppermute(value, axis, [((i + shift) % n, i) for i in range(n)])]
    all_to_all x1, blocking collectives: 34.8 us -> 28 us  [body(): lax.all_to_all(jnp.broadcast_to(local_rows[None], (zs * xs,) + local_rows...]
    all_to_all x2 -> x1, starting transfers between devices: 7.04 us -> 3.57 us  [body(): lax.all_to_all(own.reshape(zs * xs, local_tokens, feats), ('zh', 'x'), 0,...]
    ppermute x7 -> x19, starting transfers between devices: 12.4 us -> 15.4 us  [from_shift(): return lax.ppermute(value, axis, [((i + shift) % n, i) for i in range(n)])]
    convert_element_type x2 -> x3, other arithmetic: 3.16 us -> 1.07 us  [total(): return sum((part.astype(f32) for part in parts)).astype(bf16)]
    pallas_call x4 -> x6, Pallas kernels: 13 us -> 11.5 us  [the longest x3 4.9 us: logits_part(): pl.pallas_call(functools.partial(logits_kernel, counts, before is not Non...]
    unnamed x4 -> x2, local copies, waits for them, and re-layouts: 4.01 us -> 4 us
  transfers between devices with their start and end apart: 9 -> 20, of which waited for: 7 -> 9; matrix products, arithmetic and copies ran while one was open for 0% -> 3% of each run, Pallas kernels for 5% -> 7%
where the time goes in v2:
time: 152 us; the launch traced here: 151 us
  blocking collectives  52.1 us (34%)
  waiting for transfers between devices  51 us (34%)
  starting transfers between devices  19 us (12%)
  Pallas kernels  16.3 us (11%)
  other arithmetic  6.21 us (4%)
  local copies, waits for them, and re-layouts  5.72 us (4%)
    ppermute x19, waiting for transfers between devices, from_shift(): return lax.ppermute(value, axis, [((i + shift) % n, i) for i in range(n)])  34.2 us
    all_to_all x1, blocking collectives, body(): lax.all_to_all(jnp.broadcast_to(local_rows[None], (zs * xs,) + local_rows...  28 us
    all_to_all x1, blocking collectives, body(): lax.all_to_all(jnp.broadcast_to(stats[None], (devices,) + stats.shape), (...  24.1 us
    all_to_all x1, waiting for transfers between devices, body(): lax.all_to_all(own.reshape(zs * xs, local_tokens, feats), ('zh', 'x'), 0,...  16.8 us
    ppermute x19, starting transfers between devices, from_shift(): return lax.ppermute(value, axis, [((i + shift) % n, i) for i in range(n)])  15.4 us
    pallas_call x3, Pallas kernels, logits_part(): pl.pallas_call(functools.partial(logits_kernel, counts, before is not Non...  4.9 us
    unnamed x2, local copies, waits for them, and re-layouts  4 us
    pallas_call x2, Pallas kernels, products_part(): pl.pallas_call(more_products_kernel, grid=(len(blocks),), in_specs=[whole...  3.99 us
  transfers between devices with their start and end apart: 20, of which 9 were waited for; matrix products, arithmetic and copies ran while one was open for 3% of the time, Pallas kernels for 7%

profile of v2, /device:TPU:32, one launch (start us, length us, event | category | flops | bytes accessed | tf_op | source)
XLA Modules:
  0.0 151.2 jit_solution(4044445180015854019)
XLA Ops:
  0.6 0.7 broadcast_select_fusion
  1.3 0.8 fusion
  2.2 28.0 %all_to_all.15 = bf16[16,64,256]{2,1,0:T(8,128)(2,1)S(1)} all-to-all(bf16[16,64,256]{2,1,0:T(8,128)(2,1)S(1)} %broadcast_in_dim.24), channel_id=1, replica_groups=mesh['g'=2,'zh'=4,'y'=4,'c'=2,'x'=4] {'zh','x'}, dimensions={0} | all-to-all | bytes 1048576 | tf_op jit(solution)/shard_map/all_to_all | solution.py:326
  30.3 3.1 %collective-permute-start = (bf16[256,1024]{1,0:T(8,128)(2,1)S(1)}, bf16[256,1024]{1,0:T(8,128)(2,1)S(1)}, u32[]{:S(2)}, u32[]{:S(2)}) collective-permute-start(bf16[256,1024]{1,0:T(8,128)(2,1)S(1)} %pad_maximum_fusion.refs_0_), channel_id=1, source_target_pairs={{8,0},{16,8},{24,16},{0,24},{9,1},{17,9},{25,17},{1,25},{10,2},{18... | collective-permute-start | bytes 1572872 | tf_op jit(solution)/shard_map/ppermute | solution.py:22
  33.4 1.0 reshape.36.scales
  34.5 4.0 %copy-done = bf16[1,8192,640]{2,1,0:T(8,128)(2,1)S(1)} copy-done((bf16[1,8192,640]{2,1,0:T(8,128)(2,1)S(1)}, bf16[1,8192,640]{2,1,0:T(8,128)(2,1)}, u32[]{:S(2)}) %copy-start) | copy-done | bytes 10485784
  38.5 3.6 %dequantize.1 = (bf16[2,4,4,256,640]{4,3,2,1,0:T(8,128)(2,1)S(1)}, bf16[16,128]{1,0:T(8,128)(2,1)S(1)}) custom-call(s32[3]{0:T(128)S(1)} %pad_add_fusion.place, bf16[4,4,2,256,640]{4,3,2,1,0:T(8,128)(2,1)S(1)} %bitcast.21, f32[4,4,2,2,640]{4,3,2,1,0:T(2,128)S(1)} %reshape.36.scales), custom_call_target="tpu_custom_call" | custom-call | flops 5242880 | bytes 20971520 | tf_op jit(solution)/shard_map/dequantize/pallas_call | solution.py:67
  42.6 1.9 %collective-permute-done.refs_1_ = bf16[256,1024]{1,0:T(8,128)(2,1)S(1)} collective-permute-done((bf16[256,1024]{1,0:T(8,128)(2,1)S(1)}, bf16[256,1024]{1,0:T(8,128)(2,1)S(1)}, u32[]{:S(2)}, u32[]{:S(2)}) %collective-permute-start) | collective-permute-done | bytes 524320 | tf_op jit(solution)/shard_map/ppermute | solution.py:22
  44.5 3.4 %collective-permute-done.2.refs_2_ = bf16[256,1024]{1,0:T(8,128)(2,1)S(1)} collective-permute-done((bf16[256,1024]{1,0:T(8,128)(2,1)S(1)}, bf16[256,1024]{1,0:T(8,128)(2,1)S(1)}, u32[]{:S(2)}, u32[]{:S(2)}) %collective-permute-start.2) | collective-permute-done | bytes 524320 | tf_op jit(solution)/shard_map/ppermute | solution.py:22
  47.9 0.7 slice_add_fusion
  48.7 0.7 slice_add_fusion.1
  49.3 3.3 %collective-permute-start.1 = (bf16[128,1024]{1,0:T(8,128)(2,1)S(1)}, bf16[128,1024]{1,0:T(8,128)(2,1)S(1)}, u32[]{:S(2)}, u32[]{:S(2)}) collective-permute-start(bf16[128,1024]{1,0:T(8,128)(2,1)S(1)} %slice_add_fusion.1), channel_id=1, source_target_pairs={{8,0},{16,8},{24,16},{0,24},{9,1},{17,9},{25,17},{1,25},{10,2},{18... | collective-permute-start | bytes 786440 | tf_op jit(solution)/shard_map/ppermute | solution.py:22
  52.6 1.8 %logits.3.refs_4_ = f32[256,640]{1,0:T(8,128)S(1)} custom-call(bf16[256,1024]{1,0:T(8,128)(2,1)S(1)} %pad_maximum_fusion.refs_0_, bf16[256,1024]{1,0:T(8,128)(2,1)S(1)} %collective-permute-done.refs_1_, bf16[256,1024]{1,0:T(8,128)(2,1)S(1)} %collective-permute-done.2.refs_2_, bf16[2,4,1024,640]{3,2,1,0:T(8,128)(2,1)S(1)} %bitcast.15), custom_call_target="tpu_custom_call" | custom-call | flops 1006632960 | bytes 5505024 | tf_op jit(solution)/shard_map/logits/pallas_call | solution.py:156
  54.5 1.8 %logits.4.refs_5_ = f32[256,640]{1,0:T(8,128)S(1)} custom-call(bf16[256,1024]{1,0:T(8,128)(2,1)S(1)} %collective-permute-done.4.refs_0_, bf16[256,1024]{1,0:T(8,128)(2,1)S(1)} %collective-permute-done.5.refs_1_, bf16[256,1024]{1,0:T(8,128)(2,1)S(1)} %collective-permute-done.6.refs_2_, bf16[2,4,1024,640]{3,2,1,0:T(8,128)(2,1)S(1)} %bitcast.16, ...), custom_call_target="tpu_custom_call" | custom-call | flops 1006632960 | bytes 5505024 | tf_op jit(solution)/shard_map/logits/pallas_call | solution.py:156
  56.3 2.3 %collective-permute-done.3.refs_1_ = bf16[128,1024]{1,0:T(8,128)(2,1)S(1)} collective-permute-done((bf16[128,1024]{1,0:T(8,128)(2,1)S(1)}, bf16[128,1024]{1,0:T(8,128)(2,1)S(1)}, u32[]{:S(2)}, u32[]{:S(2)}) %collective-permute-start.3) | collective-permute-done | bytes 262176 | tf_op jit(solution)/shard_map/ppermute | solution.py:22
  59.1 1.0 collective-permute-done.7.refs_2_
  60.5 1.3 logits.5
  61.9 10.2 %collective-permute-done.9.received = bf16[272,640]{1,0:T(8,128)(2,1)S(1)} collective-permute-done((bf16[272,640]{1,0:T(8,128)(2,1)S(1)}, bf16[272,640]{1,0:T(8,128)(2,1)S(1)}, u32[]{:S(2)}, u32[]{:S(2)}) %collective-permute-start.9) | collective-permute-done | bytes 348192 | tf_op jit(solution)/shard_map/ppermute | solution.py:22
  72.1 1.2 local_stats.1
  73.3 24.1 %all_to_all.16.stats = f32[128,4,128]{2,1,0:T(4,128)S(1)} all-to-all(f32[128,4,128]{2,1,0:T(4,128)S(1)} %broadcast_in_dim.25), channel_id=1, replica_groups=mesh['g'=2,'zh'=4,'y'=4,'c'=2,'x'=4] {'zh','y','c','x'}, dimensions={0} | all-to-all | bytes 524288 | tf_op jit(solution)/shard_map/all_to_all | solution.py:344
  97.4 2.6 %gradient_products.1 = (bf16[256,1024]{1,0:T(8,128)(2,1)S(1)}, bf16[256,1024]{1,0:T(8,128)(2,1)S(1)}, bf16[256,640]{1,0:T(8,128)(2,1)S(1)}, f32[1,256]{1,0:T(1,128)S(1)}) custom-call(s32[3]{0:T(128)S(1)} %pad_add_fusion.place, f32[256,640]{1,0:T(8,128)S(1)} %get-tuple-element.26.own, bf16[272,640]{1,0:T(8,128)(2,1)S(1)} %collective-permute-done.9.received, ...), custom_call_target="tpu_custom_call" | custom-call | flops 671088640 | bytes 3670016 | tf_op jit(solution)/shard_map/gradient_products/pallas_call | solution.py:293
  100.3 2.0 %products.3 = (bf16[256,1024]{1,0:T(8,128)(2,1)S(1)}, bf16[256,1024]{1,0:T(8,128)(2,1)S(1)}, bf16[256,1024]{1,0:T(8,128)(2,1)S(1)}) custom-call(bf16[256,640]{1,0:T(8,128)(2,1)S(1)} %get-tuple-element.28.grad, bf16[2,4,1024,640]{3,2,1,0:T(8,128)(2,1)S(1)} %bitcast.19), custom_call_target="tpu_custom_call" | custom-call | flops 1006632960 | bytes 5505024 | tf_op jit(solution)/shard_map/products/pallas_call | solution.py:282
  103.7 2.8 %collective-permute-start.16 = (bf16[128,1024]{1,0:T(8,128)(2,1)S(1)}, bf16[128,1024]{1,0:T(8,128)(2,1)S(1)}, u32[]{:S(2)}, u32[]{:S(2)}) collective-permute-start(bf16[128,1024]{1,0:T(8,128)(2,1)S(1)} %get-tuple-element.49), channel_id=1, source_target_pairs={{8,0},{16,8},{24,16},{0,24},{9,1},{17,9},{25,17},{1,25},{10,2},{18... | collective-permute-start | bytes 786440 | tf_op jit(solution)/shard_map/ppermute | solution.py:22
  106.4 2.0 %products.2 = (bf16[256,1024]{1,0:T(8,128)(2,1)S(1)}, bf16[256,1024]{1,0:T(8,128)(2,1)S(1)}, bf16[256,1024]{1,0:T(8,128)(2,1)S(1)}) custom-call(bf16[256,640]{1,0:T(8,128)(2,1)S(1)} %get-tuple-element.28.grad, bf16[2,4,1024,640]{3,2,1,0:T(8,128)(2,1)S(1)} %bitcast.20), custom_call_target="tpu_custom_call" | custom-call | flops 1006632960 | bytes 5505024 | tf_op jit(solution)/shard_map/products/pallas_call | solution.py:282
  108.5 4.6 %collective-permute-done.13 = bf16[128,1024]{1,0:T(8,128)(2,1)S(1)} collective-permute-done((bf16[128,1024]{1,0:T(8,128)(2,1)S(1)}, bf16[128,1024]{1,0:T(8,128)(2,1)S(1)}, u32[]{:S(2)}, u32[]{:S(2)}) %collective-permute-start.13) | collective-permute-done | bytes 262176 | tf_op jit(solution)/shard_map/ppermute | solution.py:22
  113.7 3.3 %collective-permute-start.17 = (bf16[256,1024]{1,0:T(8,128)(2,1)S(1)}, bf16[256,1024]{1,0:T(8,128)(2,1)S(1)}, u32[]{:S(2)}, u32[]{:S(2)}) collective-permute-start(bf16[256,1024]{1,0:T(8,128)(2,1)S(1)} %pad_maximum_fusion.2), channel_id=1, source_target_pairs={{8,0},{16,8},{24,16},{0,24},{9,1},{17,9},{25,17},{1,25},{10,2},{18... | collective-permute-start | bytes 1572872 | tf_op jit(solution)/shard_map/ppermute | solution.py:22
  117.0 0.8 collective-permute-start.18
  117.9 10.5 %collective-permute-done.14 = bf16[256,1024]{1,0:T(8,128)(2,1)S(1)} collective-permute-done((bf16[256,1024]{1,0:T(8,128)(2,1)S(1)}, bf16[256,1024]{1,0:T(8,128)(2,1)S(1)}, u32[]{:S(2)}, u32[]{:S(2)}) %collective-permute-start.14) | collective-permute-done | bytes 524320 | tf_op jit(solution)/shard_map/ppermute | solution.py:22
  128.8 0.8 pad_maximum_fusion.3
  129.6 3.6 %all-to-all-start.2 = ((bf16[16,64,256]{2,1,0:T(8,128)(2,1)}), bf16[16,64,256]{2,1,0:T(8,128)(2,1)S(1)}, u32[]{:S(2)}, u32[]{:S(2)}) async-start(bf16[16,64,256]{2,1,0:T(8,128)(2,1)} %bitcast.11), calls=%async_computation.2 | async-start | bytes 1048576 | tf_op jit(solution)/shard_map/all_to_all | solution.py:376
  133.8 16.8 %all-to-all-done.2 = bf16[16,64,256]{2,1,0:T(8,128)(2,1)S(1)} async-done(((bf16[16,64,256]{2,1,0:T(8,128)(2,1)}), bf16[16,64,256]{2,1,0:T(8,128)(2,1)S(1)}, u32[]{:S(2)}, u32[]{:S(2)}) %all-to-all-start.2) | async-done | bytes 524320 | tf_op jit(solution)/shard_map/all_to_all | solution.py:376
  150.6 0.7 reduce_sum.12
  (41 shorter events, 5.1 us)
Async XLA Ops:
  30.3 14.2 %collective-permute-start = (bf16[256,1024]{1,0:T(8,128)(2,1)S(1)}, bf16[256,1024]{1,0:T(8,128)(2,1)S(1)}, u32[]{:S(2)}, u32[]{:S(2)}) collective-permute-start(bf16[256,1024]{1,0:T(8,128)(2,1)S(1)} %pad_maximum_fusion.refs_0_), channel_id=1, source_target_pairs={{8,0},{16,8},{24,16},{0,24},{9,1},{17,9},{25,17},{1,25},{10,2},{18... | collective-permute-start | bytes 1572872 | tf_op jit(solution)/shard_map/ppermute | solution.py:22
  33.4 14.5 %collective-permute-start.2 = (bf16[256,1024]{1,0:T(8,128)(2,1)S(1)}, bf16[256,1024]{1,0:T(8,128)(2,1)S(1)}, u32[]{:S(2)}, u32[]{:S(2)}) collective-permute-start(bf16[256,1024]{1,0:T(8,128)(2,1)S(1)} %pad_maximum_fusion.refs_0_), channel_id=1, source_target_pairs={{24,0},{0,8},{8,16},{16,24},{25,1},{1,9},{9,17},{17,25},{26,2},{2,... | collective-permute-start | bytes 1572872 | tf_op jit(solution)/shard_map/ppermute | solution.py:22
  34.5 4.0 %copy-start = (bf16[1,8192,640]{2,1,0:T(8,128)(2,1)S(1)}, bf16[1,8192,640]{2,1,0:T(8,128)(2,1)}, u32[]{:S(2)}) copy-start(bf16[1,8192,640]{2,1,0:T(8,128)(2,1)} %param.5) | copy-start | bytes 31457284
  42.6 11.8 %collective-permute-start.4 = (bf16[256,1024]{1,0:T(8,128)(2,1)S(1)}, bf16[256,1024]{1,0:T(8,128)(2,1)S(1)}, u32[]{:S(2)}, u32[]{:S(2)}) collective-permute-start(bf16[256,1024]{1,0:T(8,128)(2,1)S(1)} %pad_maximum_fusion.refs_0_), channel_id=1, source_target_pairs={{4,0},{0,4},{5,1},{1,5},{6,2},{2,6},{7,3},{3,7},{12,8},{8,12},{13,... | collective-permute-start | bytes 1572872 | tf_op jit(solution)/shard_map/ppermute | solution.py:22
  44.5 10.0 %collective-permute-start.5 = (bf16[256,1024]{1,0:T(8,128)(2,1)S(1)}, bf16[256,1024]{1,0:T(8,128)(2,1)S(1)}, u32[]{:S(2)}, u32[]{:S(2)}) collective-permute-start(bf16[256,1024]{1,0:T(8,128)(2,1)S(1)} %collective-permute-done.refs_1_), channel_id=1, source_target_pairs={{4,0},{0,4},{5,1},{1,5},{6,2},{2,6},{7,3},{3,7},{12,8},{8,12},{13,... | collective-permute-start | bytes 1572872 | tf_op jit(solution)/shard_map/ppermute | solution.py:22
  47.9 6.6 %collective-permute-start.6 = (bf16[256,1024]{1,0:T(8,128)(2,1)S(1)}, bf16[256,1024]{1,0:T(8,128)(2,1)S(1)}, u32[]{:S(2)}, u32[]{:S(2)}) collective-permute-start(bf16[256,1024]{1,0:T(8,128)(2,1)S(1)} %collective-permute-done.2.refs_2_), channel_id=1, source_target_pairs={{4,0},{0,4},{5,1},{1,5},{6,2},{2,6},{7,3},{3,7},{12,8},{8,12},{13,... | collective-permute-start | bytes 1572872 | tf_op jit(solution)/shard_map/ppermute | solution.py:22
  48.6 10.0 %collective-permute-start.3 = (bf16[128,1024]{1,0:T(8,128)(2,1)S(1)}, bf16[128,1024]{1,0:T(8,128)(2,1)S(1)}, u32[]{:S(2)}, u32[]{:S(2)}) collective-permute-start(bf16[128,1024]{1,0:T(8,128)(2,1)S(1)} %slice_add_fusion), channel_id=1, source_target_pairs={{24,0},{0,8},{8,16},{16,24},{25,1},{1,9},{9,17},{17,25},{26,2},{2,... | collective-permute-start | bytes 786440 | tf_op jit(solution)/shard_map/ppermute | solution.py:22
  49.3 9.3 %collective-permute-start.1 = (bf16[128,1024]{1,0:T(8,128)(2,1)S(1)}, bf16[128,1024]{1,0:T(8,128)(2,1)S(1)}, u32[]{:S(2)}, u32[]{:S(2)}) collective-permute-start(bf16[128,1024]{1,0:T(8,128)(2,1)S(1)} %slice_add_fusion.1), channel_id=1, source_target_pairs={{8,0},{16,8},{24,16},{0,24},{9,1},{17,9},{25,17},{1,25},{10,2},{18... | collective-permute-start | bytes 786440 | tf_op jit(solution)/shard_map/ppermute | solution.py:22
  58.6 1.5 %collective-permute-start.7 = (bf16[128,1024]{1,0:T(8,128)(2,1)S(1)}, bf16[128,1024]{1,0:T(8,128)(2,1)S(1)}, u32[]{:S(2)}, u32[]{:S(2)}) collective-permute-start(bf16[128,1024]{1,0:T(8,128)(2,1)S(1)} %collective-permute-done.1.refs_0_), channel_id=1, source_target_pairs={{4,0},{0,4},{5,1},{1,5},{6,2},{2,6},{7,3},{3,7},{12,8},{8,12},{13,... | collective-permute-start | bytes 786440 | tf_op jit(solution)/shard_map/ppermute | solution.py:22
  58.6 1.9 %collective-permute-start.8 = (bf16[128,1024]{1,0:T(8,128)(2,1)S(1)}, bf16[128,1024]{1,0:T(8,128)(2,1)S(1)}, u32[]{:S(2)}, u32[]{:S(2)}) collective-permute-start(bf16[128,1024]{1,0:T(8,128)(2,1)S(1)} %collective-permute-done.3.refs_1_), channel_id=1, source_target_pairs={{4,0},{0,4},{5,1},{1,5},{6,2},{2,6},{7,3},{3,7},{12,8},{8,12},{13,... | collective-permute-start | bytes 786440 | tf_op jit(solution)/shard_map/ppermute | solution.py:22
  61.8 10.3 %collective-permute-start.9 = (bf16[272,640]{1,0:T(8,128)(2,1)S(1)}, bf16[272,640]{1,0:T(8,128)(2,1)S(1)}, u32[]{:S(2)}, u32[]{:S(2)}) collective-permute-start(bf16[272,640]{1,0:T(8,128)(2,1)S(1)} %get-tuple-element.27), channel_id=1, source_target_pairs={{128,0},{0,128},{129,1},{1,129},{130,2},{2,130},{131,3},{3,131},{1... | collective-permute-start | bytes 1044488 | tf_op jit(solution)/shard_map/ppermute | solution.py:22
  100.1 2.8 %collective-permute-start.12 = (bf16[256,1024]{1,0:T(8,128)(2,1)S(1)}, bf16[256,1024]{1,0:T(8,128)(2,1)S(1)}, u32[]{:S(2)}, u32[]{:S(2)}) collective-permute-start(bf16[256,1024]{1,0:T(8,128)(2,1)S(1)} %get-tuple-element.34), channel_id=1, source_target_pairs={{4,0},{0,4},{5,1},{1,5},{6,2},{2,6},{7,3},{3,7},{12,8},{8,12},{13,... | collective-permute-start | bytes 1572872 | tf_op jit(solution)/shard_map/ppermute | solution.py:22
  102.3 6.2 %collective-permute-start.11 = (bf16[256,1024]{1,0:T(8,128)(2,1)S(1)}, bf16[256,1024]{1,0:T(8,128)(2,1)S(1)}, u32[]{:S(2)}, u32[]{:S(2)}) collective-permute-start(bf16[256,1024]{1,0:T(8,128)(2,1)S(1)} %get-tuple-element.32), channel_id=1, source_target_pairs={{4,0},{0,4},{5,1},{1,5},{6,2},{2,6},{7,3},{3,7},{12,8},{8,12},{13,... | collective-permute-start | bytes 1572872 | tf_op jit(solution)/shard_map/ppermute | solution.py:22
  102.7 5.7 %collective-permute-start.15 = (bf16[256,1024]{1,0:T(8,128)(2,1)S(1)}, bf16[256,1024]{1,0:T(8,128)(2,1)S(1)}, u32[]{:S(2)}, u32[]{:S(2)}) collective-permute-start(bf16[256,1024]{1,0:T(8,128)(2,1)S(1)} %get-tuple-element.36), channel_id=1, source_target_pairs={{4,0},{0,4},{5,1},{1,5},{6,2},{2,6},{7,3},{3,7},{12,8},{8,12},{13,... | collective-permute-start | bytes 1572872 | tf_op jit(solution)/shard_map/ppermute | solution.py:22
  103.1 9.9 %collective-permute-start.13 = (bf16[128,1024]{1,0:T(8,128)(2,1)S(1)}, bf16[128,1024]{1,0:T(8,128)(2,1)S(1)}, u32[]{:S(2)}, u32[]{:S(2)}) collective-permute-start(bf16[128,1024]{1,0:T(8,128)(2,1)S(1)} %get-tuple-element.48), channel_id=1, source_target_pairs={{24,0},{0,8},{8,16},{16,24},{25,1},{1,9},{9,17},{17,25},{26,2},{2,... | collective-permute-start | bytes 786440 | tf_op jit(solution)/shard_map/ppermute | solution.py:22
  103.7 9.4 %collective-permute-start.16 = (bf16[128,1024]{1,0:T(8,128)(2,1)S(1)}, bf16[128,1024]{1,0:T(8,128)(2,1)S(1)}, u32[]{:S(2)}, u32[]{:S(2)}) collective-permute-start(bf16[128,1024]{1,0:T(8,128)(2,1)S(1)} %get-tuple-element.49), channel_id=1, source_target_pairs={{8,0},{16,8},{24,16},{0,24},{9,1},{17,9},{25,17},{1,25},{10,2},{18... | collective-permute-start | bytes 786440 | tf_op jit(solution)/shard_map/ppermute | solution.py:22
  106.4 11.5 %collective-permute-start.10 = (bf16[256,1024]{1,0:T(8,128)(2,1)S(1)}, bf16[256,1024]{1,0:T(8,128)(2,1)S(1)}, u32[]{:S(2)}, u32[]{:S(2)}) collective-permute-start(bf16[256,1024]{1,0:T(8,128)(2,1)S(1)} %get-tuple-element.30), channel_id=1, source_target_pairs={{4,0},{0,4},{5,1},{1,5},{6,2},{2,6},{7,3},{3,7},{12,8},{8,12},{13,... | collective-permute-start | bytes 1572872 | tf_op jit(solution)/shard_map/ppermute | solution.py:22
  113.6 14.8 %collective-permute-start.14 = (bf16[256,1024]{1,0:T(8,128)(2,1)S(1)}, bf16[256,1024]{1,0:T(8,128)(2,1)S(1)}, u32[]{:S(2)}, u32[]{:S(2)}) collective-permute-start(bf16[256,1024]{1,0:T(8,128)(2,1)S(1)} %pad_maximum_fusion.1), channel_id=1, source_target_pairs={{24,0},{0,8},{8,16},{16,24},{25,1},{1,9},{9,17},{17,25},{26,2},{2,... | collective-permute-start | bytes 1572872 | tf_op jit(solution)/shard_map/ppermute | solution.py:22
  113.7 14.6 %collective-permute-start.17 = (bf16[256,1024]{1,0:T(8,128)(2,1)S(1)}, bf16[256,1024]{1,0:T(8,128)(2,1)S(1)}, u32[]{:S(2)}, u32[]{:S(2)}) collective-permute-start(bf16[256,1024]{1,0:T(8,128)(2,1)S(1)} %pad_maximum_fusion.2), channel_id=1, source_target_pairs={{8,0},{16,8},{24,16},{0,24},{9,1},{17,9},{25,17},{1,25},{10,2},{18... | collective-permute-start | bytes 1572872 | tf_op jit(solution)/shard_map/ppermute | solution.py:22
  117.0 11.7 %collective-permute-start.18 = (f32[1,256]{1,0:T(1,128)S(1)}, f32[1,256]{1,0:T(1,128)S(1)}, u32[]{:S(2)}, u32[]{:S(2)}) collective-permute-start(f32[1,256]{1,0:T(1,128)S(1)} %get-tuple-element.37), channel_id=1, source_target_pairs={{128,0},{0,128},{129,1},{1,129},{130,2},{2,130},{131,3},{3,131},{1... | collective-permute-start | bytes 3080 | tf_op jit(solution)/shard_map/ppermute | solution.py:22
  129.6 20.9 %all-to-all-start.2 = ((bf16[16,64,256]{2,1,0:T(8,128)(2,1)}), bf16[16,64,256]{2,1,0:T(8,128)(2,1)S(1)}, u32[]{:S(2)}, u32[]{:S(2)}) async-start(bf16[16,64,256]{2,1,0:T(8,128)(2,1)} %bitcast.11), calls=%async_computation.2 | async-start | bytes 1048576 | tf_op jit(solution)/shard_map/all_to_all | solution.py:376

commit v3 on v2

--- a/solution.py
+++ b/solution.py
@@ -263,7 +263,22 @@
     products(grad[...], weights, outs)
 
 
-def products_part(blocks, weights, tokens, grad=None, sources=None):
+def summed_products_kernel(grad, weights, *refs):
+    blocks = len(refs) // 3
+    value = lax.dot_general(
+        grad[...], weights[0, 0], (((1,), (1,)), ((), ())), preferred_element_type=f32
+    )
+    for i in range(blocks):
+        came, low, high = refs[i], refs[blocks + 2 * i], refs[blocks + 2 * i + 1]
+
+        @pl.when(pl.program_id(0) == i)
+        def _(came=came, low=low, high=high):
+            half = low.shape[0]
+            low[...] = (value[:half] + came[:half].astype(f32)).astype(bf16)
+            high[...] = (value[half:] + came[half:].astype(f32)).astype(bf16)
+
+
+def products_part(blocks, weights, tokens, grad=None, sources=None, came=()):
     _, _, depth, cols = weights.shape
     halves = [half for half, _ in blocks]
     places = [place for _, place in blocks]
@@ -278,6 +293,18 @@
         bytes_accessed=2 * len(blocks) * depth * (cols + tokens),
         transcendentals=0,
     )
+    if came:
+        part = (tokens // 2, depth)
+        return pl.pallas_call(
+            summed_products_kernel,
+            grid=(len(blocks),),
+            in_specs=[whole(grad.shape), weight_spec] + [whole(a.shape) for a in came],
+            out_specs=[whole(part)] * (2 * len(blocks)),
+            out_shape=[jax.ShapeDtypeStruct(part, bf16)] * (2 * len(blocks)),
+            compiler_params=params(24),
+            cost_estimate=cost,
+            name="summed_products",
+        )(grad, weights, *came)
     if grad is not None:
         return pl.pallas_call(
             more_products_kernel,
@@ -355,22 +382,18 @@
     )
     opposite = total(kept_2, came_2)
     came_1, came_3, came_0 = (from_shift(a, "c", 1) for a in (sent_1, sent_3, sent_0))
-    kept_1, kept_3, kept_0 = products_part(
-        [(0, 1), (0, 3), (0, 0)], weights, tokens, grad=grad
+    low_1, high_1, low_3, high_3, low_0, high_0 = products_part(
+        [(0, 1), (0, 3), (0, 0)], weights, tokens, grad=grad, came=(came_1, came_3, came_0)
     )
     half = tokens // 2
     low = from_shift(opposite[:half], "y", 3)
     high = from_shift(opposite[half:], "y", 1)
-    following = jnp.concatenate(
-        [total(kept_1[:half], came_1[:half], low), total(kept_1[half:], came_1[half:])]
-    )
-    previous = jnp.concatenate(
-        [total(kept_3[:half], came_3[:half]), total(kept_3[half:], came_3[half:], high)]
-    )
+    high_1 = from_shift(high_1, "y", 3)
+    low_3 = from_shift(low_3, "y", 1)
+    low_1 = from_shift(total(low_1, low), "y", 3)
+    high_3 = from_shift(total(high_3, high), "y", 1)
     kl_other = from_shift(kl_part, "g", 1)
-    own = total(
-        kept_0, came_0, from_shift(following, "y", 3), from_shift(previous, "y", 1)
-    )
+    own = jnp.concatenate([total(low_0, low_1, low_3), total(high_0, high_1, high_3)])
     own, kl_other = lax.optimization_barrier((own, kl_other))
     own = jnp.concatenate([own[:, z * feats : (z + 1) * feats] for z in range(zs)])
     own = lax.all_to_all(

time: 152 us -> 148 us (0.974)
  blocking collectives: 52.1 us -> 49 us
    all_to_all x1, blocking collectives: 24.1 us -> 21 us  [body(): lax.all_to_all(jnp.broadcast_to(stats[None], (devices,) + stats.shape), (...]
    pallas_call x0 -> x1, Pallas kernels: none -> 2.2 us  [products_part(): pl.pallas_call(summed_products_kernel, grid=(len(blocks),), in_specs=[who...]
    pallas_call x2 -> x1, Pallas kernels: 3.99 us -> 2 us  [products_part(): pl.pallas_call(more_products_kernel, grid=(len(blocks),), in_specs=[whole...]
    ppermute x19 -> x21, starting transfers between devices: 15.4 us -> 16.6 us  [from_shift(): return lax.ppermute(value, axis, [((i + shift) % n, i) for i in range(n)])]
    ppermute x19 -> x21, waiting for transfers between devices: 34.2 us -> 33.2 us  [from_shift(): return lax.ppermute(value, axis, [((i + shift) % n, i) for i in range(n)])]
  transfers between devices with their start and end apart: 20 -> 22, of which waited for: 9 -> 12; matrix products, arithmetic and copies ran while one was open for 3% -> 3% of each run, Pallas kernels for 7% -> 8%
where the time goes in v3:
time: 148 us
  waiting for transfers between devices  49.7 us (34%)
  blocking collectives  49 us (33%)
  starting transfers between devices  20.2 us (14%)
  Pallas kernels  16.6 us (11%)
  local copies, waits for them, and re-layouts  5.72 us (4%)
  other arithmetic  5.66 us (4%)
    ppermute x21, waiting for transfers between devices, from_shift(): return lax.ppermute(value, axis, [((i + shift) % n, i) for i in range(n)])  33.2 us
    all_to_all x1, blocking collectives, body(): lax.all_to_all(jnp.broadcast_to(local_rows[None], (zs * xs,) + local_rows...  28 us
    all_to_all x1, blocking collectives, body(): lax.all_to_all(jnp.broadcast_to(stats[None], (devices,) + stats.shape), (...  21 us
    ppermute x21, starting transfers between devices, from_shift(): return lax.ppermute(value, axis, [((i + shift) % n, i) for i in range(n)])  16.6 us
    all_to_all x1, waiting for transfers between devices, body(): lax.all_to_all(own.reshape(zs * xs, local_tokens, feats), ('zh', 'x'), 0,...  16.5 us
    pallas_call x3, Pallas kernels, logits_part(): pl.pallas_call(functools.partial(logits_kernel, counts, before is not Non...  4.92 us
    unnamed x2, local copies, waits for them, and re-layouts  4 us
    pallas_call x1, Pallas kernels, dequantize(): pl.pallas_call(dequantize_kernel, grid_spec=pltpu.PrefetchScalarGridSpec(...  3.63 us
  transfers between devices with their start and end apart: 22, of which 12 were waited for; matrix products, arithmetic and copies ran while one was open for 3% of the time, Pallas kernels for 8%

profile of v3, /device:TPU:32, one launch (start us, length us, event | category | flops | bytes accessed | tf_op | source)
XLA Modules:
  0.0 147.7 jit_solution(5142370018123326387)
XLA Ops:
  1.3 0.8 fusion
  2.2 28.0 %all_to_all.15 = bf16[16,64,256]{2,1,0:T(8,128)(2,1)S(1)} all-to-all(bf16[16,64,256]{2,1,0:T(8,128)(2,1)S(1)} %broadcast_in_dim.24), channel_id=1, replica_groups=mesh['g'=2,'zh'=4,'y'=4,'c'=2,'x'=4] {'zh','x'}, dimensions={0} | all-to-all | bytes 1048576 | tf_op jit(solution)/shard_map/all_to_all | solution.py:353
  30.3 1.7 %collective-permute-start.2 = (bf16[256,1024]{1,0:T(8,128)(2,1)S(1)}, bf16[256,1024]{1,0:T(8,128)(2,1)S(1)}, u32[]{:S(2)}, u32[]{:S(2)}) collective-permute-start(bf16[256,1024]{1,0:T(8,128)(2,1)S(1)} %pad_maximum_fusion.refs_0_), channel_id=1, source_target_pairs={{24,0},{0,8},{8,16},{16,24},{25,1},{1,9},{9,17},{17,25},{26,2},{2,... | collective-permute-start | bytes 1572872 | tf_op jit(solution)/shard_map/ppermute | solution.py:22
  31.9 1.7 %collective-permute-start = (bf16[256,1024]{1,0:T(8,128)(2,1)S(1)}, bf16[256,1024]{1,0:T(8,128)(2,1)S(1)}, u32[]{:S(2)}, u32[]{:S(2)}) collective-permute-start(bf16[256,1024]{1,0:T(8,128)(2,1)S(1)} %pad_maximum_fusion.refs_0_), channel_id=1, source_target_pairs={{8,0},{16,8},{24,16},{0,24},{9,1},{17,9},{25,17},{1,25},{10,2},{18... | collective-permute-start | bytes 1572872 | tf_op jit(solution)/shard_map/ppermute | solution.py:22
  33.6 1.0 reshape.36.scales
  34.7 4.0 %copy-done = bf16[1,8192,640]{2,1,0:T(8,128)(2,1)S(1)} copy-done((bf16[1,8192,640]{2,1,0:T(8,128)(2,1)S(1)}, bf16[1,8192,640]{2,1,0:T(8,128)(2,1)}, u32[]{:S(2)}) %copy-start) | copy-done | bytes 10485784
  38.7 3.6 %dequantize.1 = (bf16[2,4,4,256,640]{4,3,2,1,0:T(8,128)(2,1)S(1)}, bf16[16,128]{1,0:T(8,128)(2,1)S(1)}) custom-call(s32[3]{0:T(128)S(1)} %pad_add_fusion.place, bf16[4,4,2,256,640]{4,3,2,1,0:T(8,128)(2,1)S(1)} %bitcast.21, f32[4,4,2,2,640]{4,3,2,1,0:T(2,128)S(1)} %reshape.36.scales), custom_call_target="tpu_custom_call" | custom-call | flops 5242880 | bytes 20971520 | tf_op jit(solution)/shard_map/dequantize/pallas_call | solution.py:67
  42.8 2.4 %collective-permute-done.2.refs_2_ = bf16[256,1024]{1,0:T(8,128)(2,1)S(1)} collective-permute-done((bf16[256,1024]{1,0:T(8,128)(2,1)S(1)}, bf16[256,1024]{1,0:T(8,128)(2,1)S(1)}, u32[]{:S(2)}, u32[]{:S(2)}) %collective-permute-start.2) | collective-permute-done | bytes 524320 | tf_op jit(solution)/shard_map/ppermute | solution.py:22
  46.4 2.6 %collective-permute-start.1 = (bf16[128,1024]{1,0:T(8,128)(2,1)S(1)}, bf16[128,1024]{1,0:T(8,128)(2,1)S(1)}, u32[]{:S(2)}, u32[]{:S(2)}) collective-permute-start(bf16[128,1024]{1,0:T(8,128)(2,1)S(1)} %slice_add_fusion.1), channel_id=1, source_target_pairs={{8,0},{16,8},{24,16},{0,24},{9,1},{17,9},{25,17},{1,25},{10,2},{18... | collective-permute-start | bytes 786440 | tf_op jit(solution)/shard_map/ppermute | solution.py:22
  49.8 1.8 %logits.3.refs_4_ = f32[256,640]{1,0:T(8,128)S(1)} custom-call(bf16[256,1024]{1,0:T(8,128)(2,1)S(1)} %pad_maximum_fusion.refs_0_, bf16[256,1024]{1,0:T(8,128)(2,1)S(1)} %collective-permute-done.refs_1_, bf16[256,1024]{1,0:T(8,128)(2,1)S(1)} %collective-permute-done.2.refs_2_, bf16[2,4,1024,640]{3,2,1,0:T(8,128)(2,1)S(1)} %bitcast.15), custom_call_target="tpu_custom_call" | custom-call | flops 1006632960 | bytes 5505024 | tf_op jit(solution)/shard_map/logits/pallas_call | solution.py:156
  51.6 1.8 %logits.4.refs_5_ = f32[256,640]{1,0:T(8,128)S(1)} custom-call(bf16[256,1024]{1,0:T(8,128)(2,1)S(1)} %collective-permute-done.4.refs_0_, bf16[256,1024]{1,0:T(8,128)(2,1)S(1)} %collective-permute-done.5.refs_1_, bf16[256,1024]{1,0:T(8,128)(2,1)S(1)} %collective-permute-done.6.refs_2_, bf16[2,4,1024,640]{3,2,1,0:T(8,128)(2,1)S(1)} %bitcast.16, ...), custom_call_target="tpu_custom_call" | custom-call | flops 1006632960 | bytes 5505024 | tf_op jit(solution)/shard_map/logits/pallas_call | solution.py:156
  53.5 1.8 %collective-permute-done.1.refs_0_ = bf16[128,1024]{1,0:T(8,128)(2,1)S(1)} collective-permute-done((bf16[128,1024]{1,0:T(8,128)(2,1)S(1)}, bf16[128,1024]{1,0:T(8,128)(2,1)S(1)}, u32[]{:S(2)}, u32[]{:S(2)}) %collective-permute-start.1) | collective-permute-done | bytes 262176 | tf_op jit(solution)/shard_map/ppermute | solution.py:22
  55.3 4.2 %collective-permute-done.3.refs_1_ = bf16[128,1024]{1,0:T(8,128)(2,1)S(1)} collective-permute-done((bf16[128,1024]{1,0:T(8,128)(2,1)S(1)}, bf16[128,1024]{1,0:T(8,128)(2,1)S(1)}, u32[]{:S(2)}, u32[]{:S(2)}) %collective-permute-start.3) | collective-permute-done | bytes 262176 | tf_op jit(solution)/shard_map/ppermute | solution.py:22
  59.9 1.0 collective-permute-done.7.refs_2_
  61.3 1.3 logits.5
  62.7 10.2 %collective-permute-done.9.received = bf16[272,640]{1,0:T(8,128)(2,1)S(1)} collective-permute-done((bf16[272,640]{1,0:T(8,128)(2,1)S(1)}, bf16[272,640]{1,0:T(8,128)(2,1)S(1)}, u32[]{:S(2)}, u32[]{:S(2)}) %collective-permute-start.9) | collective-permute-done | bytes 348192 | tf_op jit(solution)/shard_map/ppermute | solution.py:22
  72.9 1.2 local_stats.1
  74.1 21.0 %all_to_all.16.stats = f32[128,4,128]{2,1,0:T(4,128)S(1)} all-to-all(f32[128,4,128]{2,1,0:T(4,128)S(1)} %broadcast_in_dim.25), channel_id=1, replica_groups=mesh['g'=2,'zh'=4,'y'=4,'c'=2,'x'=4] {'zh','y','c','x'}, dimensions={0} | all-to-all | bytes 524288 | tf_op jit(solution)/shard_map/all_to_all | solution.py:371
  95.1 2.7 %gradient_products.1 = (bf16[256,1024]{1,0:T(8,128)(2,1)S(1)}, bf16[256,1024]{1,0:T(8,128)(2,1)S(1)}, bf16[256,640]{1,0:T(8,128)(2,1)S(1)}, f32[1,256]{1,0:T(1,128)S(1)}) custom-call(s32[3]{0:T(128)S(1)} %pad_add_fusion.place, f32[256,640]{1,0:T(8,128)S(1)} %get-tuple-element.29.own, bf16[272,640]{1,0:T(8,128)(2,1)S(1)} %collective-permute-done.9.received, ...), custom_call_target="tpu_custom_call" | custom-call | flops 671088640 | bytes 3670016 | tf_op jit(solution)/shard_map/gradient_products/pallas_call | solution.py:320
  98.0 2.0 %products.1 = (bf16[256,1024]{1,0:T(8,128)(2,1)S(1)}, bf16[256,1024]{1,0:T(8,128)(2,1)S(1)}, bf16[256,1024]{1,0:T(8,128)(2,1)S(1)}) custom-call(bf16[256,640]{1,0:T(8,128)(2,1)S(1)} %get-tuple-element.31.grad, bf16[2,4,1024,640]{3,2,1,0:T(8,128)(2,1)S(1)} %bitcast.19), custom_call_target="tpu_custom_call" | custom-call | flops 1006632960 | bytes 5505024 | tf_op jit(solution)/shard_map/products/pallas_call | solution.py:309
  101.8 2.8 %collective-permute-start.18 = (bf16[128,1024]{1,0:T(8,128)(2,1)S(1)}, bf16[128,1024]{1,0:T(8,128)(2,1)S(1)}, u32[]{:S(2)}, u32[]{:S(2)}) collective-permute-start(bf16[128,1024]{1,0:T(8,128)(2,1)S(1)} %get-tuple-element.51), channel_id=1, source_target_pairs={{8,0},{16,8},{24,16},{0,24},{9,1},{17,9},{25,17},{1,25},{10,2},{18... | collective-permute-start | bytes 786440 | tf_op jit(solution)/shard_map/ppermute | solution.py:22
  104.6 2.2 %summed_products.1 = (bf16[128,1024]{1,0:T(8,128)(2,1)S(1)}, bf16[128,1024]{1,0:T(8,128)(2,1)S(1)}, bf16[128,1024]{1,0:T(8,128)(2,1)S(1)}, bf16[128,1024]{1,0:T(...) custom-call(bf16[256,640]{1,0:T(8,128)(2,1)S(1)} %get-tuple-element.31.grad, ...), custom_call_target="tpu_custom_call" | custom-call | flops 1006632960 | bytes 5505024 | tf_op jit(solution)/shard_map/summed_products/pallas_call | solution.py:298
  107.0 3.9 %collective-permute-done.14 = bf16[128,1024]{1,0:T(8,128)(2,1)S(1)} collective-permute-done((bf16[128,1024]{1,0:T(8,128)(2,1)S(1)}, bf16[128,1024]{1,0:T(8,128)(2,1)S(1)}, u32[]{:S(2)}, u32[]{:S(2)}) %collective-permute-start.14) | collective-permute-done | bytes 262176 | tf_op jit(solution)/shard_map/ppermute | solution.py:22
  111.3 3.8 %collective-permute-start.19 = (bf16[128,1024]{1,0:T(8,128)(2,1)S(1)}, bf16[128,1024]{1,0:T(8,128)(2,1)S(1)}, u32[]{:S(2)}, u32[]{:S(2)}) collective-permute-start(bf16[128,1024]{1,0:T(8,128)(2,1)S(1)} %add_convert_fusion.2), channel_id=1, source_target_pairs={{8,0},{16,8},{24,16},{0,24},{9,1},{17,9},{25,17},{1,25},{10,2},{18... | collective-permute-start | bytes 786440 | tf_op jit(solution)/shard_map/ppermute | solution.py:22
  115.1 0.9 collective-permute-start.20
  116.0 0.9 collective-permute-done.16
  116.9 4.6 %collective-permute-done.15 = bf16[128,1024]{1,0:T(8,128)(2,1)S(1)} collective-permute-done((bf16[128,1024]{1,0:T(8,128)(2,1)S(1)}, bf16[128,1024]{1,0:T(8,128)(2,1)S(1)}, u32[]{:S(2)}, u32[]{:S(2)}) %collective-permute-start.15) | collective-permute-done | bytes 262176 | tf_op jit(solution)/shard_map/ppermute | solution.py:22
  121.6 3.7 %collective-permute-done.17 = bf16[128,1024]{1,0:T(8,128)(2,1)S(1)} collective-permute-done((bf16[128,1024]{1,0:T(8,128)(2,1)S(1)}, bf16[128,1024]{1,0:T(8,128)(2,1)S(1)}, u32[]{:S(2)}, u32[]{:S(2)}) %collective-permute-start.17) | collective-permute-done | bytes 262176 | tf_op jit(solution)/shard_map/ppermute | solution.py:22
  125.5 0.8 pad_maximum_fusion.2
  126.4 3.6 %all-to-all-start.2 = ((bf16[16,64,256]{2,1,0:T(8,128)(2,1)}), bf16[16,64,256]{2,1,0:T(8,128)(2,1)S(1)}, u32[]{:S(2)}, u32[]{:S(2)}) async-start(bf16[16,64,256]{2,1,0:T(8,128)(2,1)} %bitcast.11), calls=%async_computation.2 | async-start | bytes 1048576 | tf_op jit(solution)/shard_map/all_to_all | solution.py:399
  130.5 16.5 %all-to-all-done.2 = bf16[16,64,256]{2,1,0:T(8,128)(2,1)S(1)} async-done(((bf16[16,64,256]{2,1,0:T(8,128)(2,1)}), bf16[16,64,256]{2,1,0:T(8,128)(2,1)S(1)}, u32[]{:S(2)}, u32[]{:S(2)}) %all-to-all-start.2) | async-done | bytes 524320 | tf_op jit(solution)/shard_map/all_to_all | solution.py:399
  147.0 0.7 reduce_sum.12
  (46 shorter events, 7.9 us)
Async XLA Ops:
  30.3 15.0 %collective-permute-start.2 = (bf16[256,1024]{1,0:T(8,128)(2,1)S(1)}, bf16[256,1024]{1,0:T(8,128)(2,1)S(1)}, u32[]{:S(2)}, u32[]{:S(2)}) collective-permute-start(bf16[256,1024]{1,0:T(8,128)(2,1)S(1)} %pad_maximum_fusion.refs_0_), channel_id=1, source_target_pairs={{24,0},{0,8},{8,16},{16,24},{25,1},{1,9},{9,17},{17,25},{26,2},{2,... | collective-permute-start | bytes 1572872 | tf_op jit(solution)/shard_map/ppermute | solution.py:22
  31.9 13.3 %collective-permute-start = (bf16[256,1024]{1,0:T(8,128)(2,1)S(1)}, bf16[256,1024]{1,0:T(8,128)(2,1)S(1)}, u32[]{:S(2)}, u32[]{:S(2)}) collective-permute-start(bf16[256,1024]{1,0:T(8,128)(2,1)S(1)} %pad_maximum_fusion.refs_0_), channel_id=1, source_target_pairs={{8,0},{16,8},{24,16},{0,24},{9,1},{17,9},{25,17},{1,25},{10,2},{18... | collective-permute-start | bytes 1572872 | tf_op jit(solution)/shard_map/ppermute | solution.py:22
  34.7 4.0 %copy-start = (bf16[1,8192,640]{2,1,0:T(8,128)(2,1)S(1)}, bf16[1,8192,640]{2,1,0:T(8,128)(2,1)}, u32[]{:S(2)}) copy-start(bf16[1,8192,640]{2,1,0:T(8,128)(2,1)} %param.5) | copy-start | bytes 31457284
  42.8 8.8 %collective-permute-start.4 = (bf16[256,1024]{1,0:T(8,128)(2,1)S(1)}, bf16[256,1024]{1,0:T(8,128)(2,1)S(1)}, u32[]{:S(2)}, u32[]{:S(2)}) collective-permute-start(bf16[256,1024]{1,0:T(8,128)(2,1)S(1)} %pad_maximum_fusion.refs_0_), channel_id=1, source_target_pairs={{4,0},{0,4},{5,1},{1,5},{6,2},{2,6},{7,3},{3,7},{12,8},{8,12},{13,... | collective-permute-start | bytes 1572872 | tf_op jit(solution)/shard_map/ppermute | solution.py:22
  45.2 6.4 %collective-permute-start.6 = (bf16[256,1024]{1,0:T(8,128)(2,1)S(1)}, bf16[256,1024]{1,0:T(8,128)(2,1)S(1)}, u32[]{:S(2)}, u32[]{:S(2)}) collective-permute-start(bf16[256,1024]{1,0:T(8,128)(2,1)S(1)} %collective-permute-done.2.refs_2_), channel_id=1, source_target_pairs={{4,0},{0,4},{5,1},{1,5},{6,2},{2,6},{7,3},{3,7},{12,8},{8,12},{13,... | collective-permute-start | bytes 1572872 | tf_op jit(solution)/shard_map/ppermute | solution.py:22
  45.3 6.4 %collective-permute-start.5 = (bf16[256,1024]{1,0:T(8,128)(2,1)S(1)}, bf16[256,1024]{1,0:T(8,128)(2,1)S(1)}, u32[]{:S(2)}, u32[]{:S(2)}) collective-permute-start(bf16[256,1024]{1,0:T(8,128)(2,1)S(1)} %collective-permute-done.refs_1_), channel_id=1, source_target_pairs={{4,0},{0,4},{5,1},{1,5},{6,2},{2,6},{7,3},{3,7},{12,8},{8,12},{13,... | collective-permute-start | bytes 1572872 | tf_op jit(solution)/shard_map/ppermute | solution.py:22
  46.4 8.8 %collective-permute-start.1 = (bf16[128,1024]{1,0:T(8,128)(2,1)S(1)}, bf16[128,1024]{1,0:T(8,128)(2,1)S(1)}, u32[]{:S(2)}, u32[]{:S(2)}) collective-permute-start(bf16[128,1024]{1,0:T(8,128)(2,1)S(1)} %slice_add_fusion.1), channel_id=1, source_target_pairs={{8,0},{16,8},{24,16},{0,24},{9,1},{17,9},{25,17},{1,25},{10,2},{18... | collective-permute-start | bytes 786440 | tf_op jit(solution)/shard_map/ppermute | solution.py:22
  49.7 9.7 %collective-permute-start.3 = (bf16[128,1024]{1,0:T(8,128)(2,1)S(1)}, bf16[128,1024]{1,0:T(8,128)(2,1)S(1)}, u32[]{:S(2)}, u32[]{:S(2)}) collective-permute-start(bf16[128,1024]{1,0:T(8,128)(2,1)S(1)} %slice_add_fusion), channel_id=1, source_target_pairs={{24,0},{0,8},{8,16},{16,24},{25,1},{1,9},{9,17},{17,25},{26,2},{2,... | collective-permute-start | bytes 786440 | tf_op jit(solution)/shard_map/ppermute | solution.py:22
  59.4 1.5 %collective-permute-start.7 = (bf16[128,1024]{1,0:T(8,128)(2,1)S(1)}, bf16[128,1024]{1,0:T(8,128)(2,1)S(1)}, u32[]{:S(2)}, u32[]{:S(2)}) collective-permute-start(bf16[128,1024]{1,0:T(8,128)(2,1)S(1)} %collective-permute-done.1.refs_0_), channel_id=1, source_target_pairs={{4,0},{0,4},{5,1},{1,5},{6,2},{2,6},{7,3},{3,7},{12,8},{8,12},{13,... | collective-permute-start | bytes 786440 | tf_op jit(solution)/shard_map/ppermute | solution.py:22
  59.4 1.9 %collective-permute-start.8 = (bf16[128,1024]{1,0:T(8,128)(2,1)S(1)}, bf16[128,1024]{1,0:T(8,128)(2,1)S(1)}, u32[]{:S(2)}, u32[]{:S(2)}) collective-permute-start(bf16[128,1024]{1,0:T(8,128)(2,1)S(1)} %collective-permute-done.3.refs_1_), channel_id=1, source_target_pairs={{4,0},{0,4},{5,1},{1,5},{6,2},{2,6},{7,3},{3,7},{12,8},{8,12},{13,... | collective-permute-start | bytes 786440 | tf_op jit(solution)/shard_map/ppermute | solution.py:22
  62.6 10.3 %collective-permute-start.9 = (bf16[272,640]{1,0:T(8,128)(2,1)S(1)}, bf16[272,640]{1,0:T(8,128)(2,1)S(1)}, u32[]{:S(2)}, u32[]{:S(2)}) collective-permute-start(bf16[272,640]{1,0:T(8,128)(2,1)S(1)} %get-tuple-element.30), channel_id=1, source_target_pairs={{128,0},{0,128},{129,1},{1,129},{130,2},{2,130},{131,3},{3,131},{1... | collective-permute-start | bytes 1044488 | tf_op jit(solution)/shard_map/ppermute | solution.py:22
  97.8 3.2 %collective-permute-start.13 = (bf16[256,1024]{1,0:T(8,128)(2,1)S(1)}, bf16[256,1024]{1,0:T(8,128)(2,1)S(1)}, u32[]{:S(2)}, u32[]{:S(2)}) collective-permute-start(bf16[256,1024]{1,0:T(8,128)(2,1)S(1)} %get-tuple-element.38), channel_id=1, source_target_pairs={{4,0},{0,4},{5,1},{1,5},{6,2},{2,6},{7,3},{3,7},{12,8},{8,12},{13,... | collective-permute-start | bytes 1572872 | tf_op jit(solution)/shard_map/ppermute | solution.py:22
  100.0 4.6 %collective-permute-start.10 = (bf16[256,1024]{1,0:T(8,128)(2,1)S(1)}, bf16[256,1024]{1,0:T(8,128)(2,1)S(1)}, u32[]{:S(2)}, u32[]{:S(2)}) collective-permute-start(bf16[256,1024]{1,0:T(8,128)(2,1)S(1)} %get-tuple-element.32), channel_id=1, source_target_pairs={{4,0},{0,4},{5,1},{1,5},{6,2},{2,6},{7,3},{3,7},{12,8},{8,12},{13,... | collective-permute-start | bytes 1572872 | tf_op jit(solution)/shard_map/ppermute | solution.py:22
  100.5 4.1 %collective-permute-start.11 = (bf16[256,1024]{1,0:T(8,128)(2,1)S(1)}, bf16[256,1024]{1,0:T(8,128)(2,1)S(1)}, u32[]{:S(2)}, u32[]{:S(2)}) collective-permute-start(bf16[256,1024]{1,0:T(8,128)(2,1)S(1)} %get-tuple-element.33), channel_id=1, source_target_pairs={{4,0},{0,4},{5,1},{1,5},{6,2},{2,6},{7,3},{3,7},{12,8},{8,12},{13,... | collective-permute-start | bytes 1572872 | tf_op jit(solution)/shard_map/ppermute | solution.py:22
  100.6 4.0 %collective-permute-start.12 = (bf16[256,1024]{1,0:T(8,128)(2,1)S(1)}, bf16[256,1024]{1,0:T(8,128)(2,1)S(1)}, u32[]{:S(2)}, u32[]{:S(2)}) collective-permute-start(bf16[256,1024]{1,0:T(8,128)(2,1)S(1)} %get-tuple-element.34), channel_id=1, source_target_pairs={{4,0},{0,4},{5,1},{1,5},{6,2},{2,6},{7,3},{3,7},{12,8},{8,12},{13,... | collective-permute-start | bytes 1572872 | tf_op jit(solution)/shard_map/ppermute | solution.py:22
  101.2 9.6 %collective-permute-start.14 = (bf16[128,1024]{1,0:T(8,128)(2,1)S(1)}, bf16[128,1024]{1,0:T(8,128)(2,1)S(1)}, u32[]{:S(2)}, u32[]{:S(2)}) collective-permute-start(bf16[128,1024]{1,0:T(8,128)(2,1)S(1)} %get-tuple-element.50), channel_id=1, source_target_pairs={{24,0},{0,8},{8,16},{16,24},{25,1},{1,9},{9,17},{17,25},{26,2},{2,... | collective-permute-start | bytes 786440 | tf_op jit(solution)/shard_map/ppermute | solution.py:22
  101.8 9.5 %collective-permute-start.18 = (bf16[128,1024]{1,0:T(8,128)(2,1)S(1)}, bf16[128,1024]{1,0:T(8,128)(2,1)S(1)}, u32[]{:S(2)}, u32[]{:S(2)}) collective-permute-start(bf16[128,1024]{1,0:T(8,128)(2,1)S(1)} %get-tuple-element.51), channel_id=1, source_target_pairs={{8,0},{16,8},{24,16},{0,24},{9,1},{17,9},{25,17},{1,25},{10,2},{18... | collective-permute-start | bytes 786440 | tf_op jit(solution)/shard_map/ppermute | solution.py:22
  106.8 10.1 %collective-permute-start.16 = (bf16[128,1024]{1,0:T(8,128)(2,1)S(1)}, bf16[128,1024]{1,0:T(8,128)(2,1)S(1)}, u32[]{:S(2)}, u32[]{:S(2)}) collective-permute-start(bf16[128,1024]{1,0:T(8,128)(2,1)S(1)} %get-tuple-element.39), channel_id=1, source_target_pairs={{8,0},{16,8},{24,16},{0,24},{9,1},{17,9},{25,17},{1,25},{10,2},{18... | collective-permute-start | bytes 786440 | tf_op jit(solution)/shard_map/ppermute | solution.py:22
  110.9 10.5 %collective-permute-start.15 = (bf16[128,1024]{1,0:T(8,128)(2,1)S(1)}, bf16[128,1024]{1,0:T(8,128)(2,1)S(1)}, u32[]{:S(2)}, u32[]{:S(2)}) collective-permute-start(bf16[128,1024]{1,0:T(8,128)(2,1)S(1)} %add_convert_fusion.4), channel_id=1, source_target_pairs={{24,0},{0,8},{8,16},{16,24},{25,1},{1,9},{9,17},{17,25},{26,2},{2,... | collective-permute-start | bytes 786440 | tf_op jit(solution)/shard_map/ppermute | solution.py:22
  111.0 14.3 %collective-permute-start.17 = (bf16[128,1024]{1,0:T(8,128)(2,1)S(1)}, bf16[128,1024]{1,0:T(8,128)(2,1)S(1)}, u32[]{:S(2)}, u32[]{:S(2)}) collective-permute-start(bf16[128,1024]{1,0:T(8,128)(2,1)S(1)} %get-tuple-element.41), channel_id=1, source_target_pairs={{24,0},{0,8},{8,16},{16,24},{25,1},{1,9},{9,17},{17,25},{26,2},{2,... | collective-permute-start | bytes 786440 | tf_op jit(solution)/shard_map/ppermute | solution.py:22
  111.3 14.0 %collective-permute-start.19 = (bf16[128,1024]{1,0:T(8,128)(2,1)S(1)}, bf16[128,1024]{1,0:T(8,128)(2,1)S(1)}, u32[]{:S(2)}, u32[]{:S(2)}) collective-permute-start(bf16[128,1024]{1,0:T(8,128)(2,1)S(1)} %add_convert_fusion.2), channel_id=1, source_target_pairs={{8,0},{16,8},{24,16},{0,24},{9,1},{17,9},{25,17},{1,25},{10,2},{18... | collective-permute-start | bytes 786440 | tf_op jit(solution)/shard_map/ppermute | solution.py:22
  115.1 10.4 %collective-permute-start.20 = (f32[1,256]{1,0:T(1,128)S(1)}, f32[1,256]{1,0:T(1,128)S(1)}, u32[]{:S(2)}, u32[]{:S(2)}) collective-permute-start(f32[1,256]{1,0:T(1,128)S(1)} %get-tuple-element.43), channel_id=1, source_target_pairs={{128,0},{0,128},{129,1},{1,129},{130,2},{2,130},{131,3},{3,131},{1... | collective-permute-start | bytes 3080 | tf_op jit(solution)/shard_map/ppermute | solution.py:22
  126.4 20.6 %all-to-all-start.2 = ((bf16[16,64,256]{2,1,0:T(8,128)(2,1)}), bf16[16,64,256]{2,1,0:T(8,128)(2,1)S(1)}, u32[]{:S(2)}, u32[]{:S(2)}) async-start(bf16[16,64,256]{2,1,0:T(8,128)(2,1)} %bitcast.11), calls=%async_computation.2 | async-start | bytes 1048576 | tf_op jit(solution)/shard_map/all_to_all | solution.py:399
